TPU v7x, 32 devices: a whole 2x2x4 slice. The times are simulated.
32 devices in a mesh: seq: 8 (over z, x), head: 4 (over y, core).
Axes of the slice: x: 2, y: 2, z: 4, core: 2. Of those that a mesh axis runs over, the one named last changes fastest.
Arguments:
- hidden: bfloat16 [2048, 2560], P(('seq', 'head')), may hold values from -6 to 6
- w_values: bfloat16 [2560, 2560], P('seq', 'head'), may hold values from -0.125 to 0.125
- w_gates: bfloat16 [2560, 2560], P('seq', 'head'), may hold values from -0.125 to 0.125
- w_steps: bfloat16 [2560, 40], P('seq', 'head'), may hold values from -0.0625 to 0.0625
- w_states: bfloat16 [2560, 256], P('seq'), may hold values from -0.125 to 0.125
- conv_weight: float32 [4, 2816], replicated, may hold values from -3 to 3
- conv_bias: float32 [2816], replicated, may hold values from -3 to 3
- step_bias: float32 [40], P('head'), may hold values from -1 to 0.5
- decay_rate: float32 [40], P('head'), may hold values from 0 to 1, as said below
- skip_gain: float32 [40], P('head'), may hold values from 1 to 8
- norm_gain: float32 [2560], replicated, may hold values from 0.5 to 1.5
- lengths: int32 [4], replicated, may hold values from 256 to 768, as said below
Outputs:
- gated_out: bfloat16 [2048, 2560], P(('seq', 'head'))
- final_states: float32 [8, 40, 64, 128], P('seq', 'head')
Inputs may be any that keep to these rules, and one draw needn't show every extreme that they name: Prompts are packed in order, each holding 256 to 768 tokens; the lengths sum to 2048. `decay_rate`: positive rates.
All inputs are finite; a program needn't handle non-finite values.
Results may differ from a plain program's by a relative error of at most 0.01.
Values may be sent and summed in bfloat16 or wider, within the bound.
A program may use at most 128 MiB of HBM per device.

v0:
```python
import jax
import jax.numpy as jnp
from jax import lax
from jax.sharding import PartitionSpec as P

STRETCH = 256


epsilon = 1e-05


def from_behind(block, axis, distance):
    devices = range(lax.axis_size(axis))
    route = [(i - distance, i) for i in devices if i - distance in devices]
    return lax.ppermute(block, axis, route)


def prefix(value, axis, join, neutral):
    place = lax.axis_index(axis)
    gathered = jax.tree.map(
        lambda a, kind: lax.all_gather(a.astype(kind), axis), value, (jnp.bfloat16, jnp.bfloat16)
    )
    state = jax.tree.map(lambda a, e: jnp.zeros_like(a) + jnp.asarray(e, a.dtype), value, neutral)

    def one(turn, state):
        return join(
            state,
            jax.tree.map(
                lambda a, own: lax.dynamic_index_in_dim(a, turn, 0, False).astype(own.dtype),
                gathered,
                value,
            ),
        )

    return lax.fori_loop(0, place, one, state)


def segments_at(positions, prompt_ends):
    counted = jnp.sum((prompt_ends[None, :] <= positions[:, None]).astype(jnp.int32), axis=1)
    return jnp.where(positions < 0, -1, counted)


def on_device(
    hidden,
    w_values,
    w_gates,
    w_steps,
    w_states,
    conv_weight,
    conv_bias,
    step_bias,
    decay_rate,
    skip_gain,
    norm_gain,
    lengths,
):
    groups = lax.axis_size("head")
    group_index = lax.axis_index("head")
    block_index = lax.axis_index("seq")
    local_width = w_values.shape[1]
    inner_width = local_width * groups
    local_heads = decay_rate.shape[0]
    head_width = local_width // local_heads
    state_width = w_states.shape[1] // 2
    conv_taps = conv_weight.shape[0]
    prompt_ends = jnp.cumsum(lengths)
    block_hidden = lax.all_gather(hidden, "head", axis=0, tiled=True)
    block_rows = block_hidden.shape[0]
    sub_rows = block_rows // groups

    def contract(piece):
        return jnp.dot(block_hidden, piece, preferred_element_type=jnp.float32)

    pieces = (
        lax.all_gather(w_values, "seq", axis=0, tiled=True),
        lax.all_gather(w_states, "seq", axis=0, tiled=True),
        lax.all_gather(w_steps, "seq", axis=0, tiled=True),
        lax.all_gather(w_gates, "seq", axis=0, tiled=True),
    )
    values_sum, states_sum, steps_sum, gates_sum = tuple((contract(piece) for piece in pieces))
    pre_rows = jnp.concatenate(
        [values_sum.astype(jnp.bfloat16), states_sum.astype(jnp.bfloat16)], axis=1
    )
    local_taps = jnp.concatenate(
        [
            lax.dynamic_slice_in_dim(conv_weight, group_index * local_width, local_width, 1),
            conv_weight[:, inner_width:],
        ],
        axis=1,
    )
    local_bias = jnp.concatenate(
        [
            lax.dynamic_slice_in_dim(conv_bias, group_index * local_width, local_width, 0),
            conv_bias[inner_width:],
        ],
        axis=0,
    )
    block_start = block_index * block_rows
    rim_rows = pre_rows[block_rows - (conv_taps - 1) :]
    prior_rim = from_behind(rim_rows, "seq", 1)
    extended = jnp.concatenate([prior_rim, pre_rows], axis=0)
    ext_positions = (
        block_start - (conv_taps - 1) + jnp.arange(block_rows + conv_taps - 1, dtype=jnp.int32)
    )
    ext_ids = segments_at(ext_positions, prompt_ends)
    own_ids = ext_ids[conv_taps - 1 :]
    filtered = jnp.zeros(pre_rows.shape, jnp.float32) + local_bias[None, :]
    for offset in range(conv_taps):
        matches = (ext_ids[offset : offset + block_rows] == own_ids).astype(jnp.float32)
        filtered = (
            filtered
            + local_taps[offset][None, :]
            * extended[offset : offset + block_rows].astype(jnp.float32)
            * matches[:, None]
        )
    conv_out = jax.nn.silu(filtered).astype(jnp.bfloat16)
    head_values = conv_out[:, :local_width]
    both_states = conv_out[:, local_width:]
    stretch_rows = STRETCH
    stretches = block_rows // stretch_rows
    positions = block_start + jnp.arange(block_rows, dtype=jnp.int32)
    segment_ids = segments_at(positions, prompt_ends)
    next_ids = segments_at(positions + 1, prompt_ends)
    before_ids = segments_at(positions - 1, prompt_ends)
    stretch_ids = segment_ids.reshape(stretches, stretch_rows)
    prior_ids = before_ids.reshape(stretches, stretch_rows)[:, 0]
    ends_mask = (segment_ids != next_ids).reshape(stretches, stretch_rows)
    step_sizes = jax.nn.softplus(steps_sum + step_bias[None, :])
    decay_steps = step_sizes * decay_rate[None, :]
    log_decay = -jnp.cumsum(decay_steps.reshape(stretches, stretch_rows, local_heads), axis=1)
    decay_heads = jnp.swapaxes(log_decay, 1, 2)
    step_heads = jnp.swapaxes(step_sizes.reshape(stretches, stretch_rows, local_heads), 1, 2)
    values = head_values.reshape(stretches, stretch_rows, local_heads, head_width)
    write_state = both_states[:, :state_width].reshape(stretches, stretch_rows, state_width)
    read_state = both_states[:, state_width:].reshape(stretches, stretch_rows, state_width)
    intersection = jnp.einsum(
        "ctn,csn->cts", read_state, write_state, preferred_element_type=jnp.float32
    )
    token_order = jnp.arange(stretch_rows, dtype=jnp.int32)
    causal = token_order[:, None] >= token_order[None, :]
    allowed = causal[None] & (stretch_ids[:, :, None] == stretch_ids[:, None, :])
    spread = decay_heads[:, :, :, None] - decay_heads[:, :, None, :]
    weights = (
        jnp.where(allowed[:, None], jnp.exp(jnp.minimum(spread, 0.0)), 0.0)
        * step_heads[:, :, None, :]
    )
    scores = (intersection[:, None] * weights).astype(jnp.bfloat16)
    within_stretch = jnp.einsum(
        "chts,cshp->cthp", scores, values, preferred_element_type=jnp.float32
    )
    last_ids = stretch_ids[:, -1]
    tail_decay = decay_heads[:, :, -1:]
    keep_tail = (stretch_ids == last_ids[:, None])[:, None, :]
    tail_coef = (
        jnp.where(keep_tail, jnp.exp(jnp.minimum(tail_decay - decay_heads, 0.0)), 0.0) * step_heads
    )
    tail_rows = (values.astype(jnp.float32) * jnp.swapaxes(tail_coef, 1, 2)[:, :, :, None]).astype(
        jnp.bfloat16
    )
    stretch_states = jnp.einsum(
        "clhp,cln->chpn", tail_rows, write_state, preferred_element_type=jnp.float32
    )
    stretch_gates = (
        jnp.exp(decay_heads[:, :, -1]) * (last_ids == prior_ids).astype(jnp.float32)[:, None]
    )
    block_gate = jnp.ones((local_heads,), jnp.float32)
    block_state = jnp.zeros((local_heads, head_width, state_width), jnp.float32)
    block_state = stretch_gates[0][:, None, None] * block_state + stretch_states[0]
    block_gate = block_gate * stretch_gates[0]

    def compose(earlier, later):
        return (earlier[0] * later[0], later[0][:, None, None] * earlier[1] + later[1])

    identity_pair = (jnp.ones_like(block_gate), jnp.zeros_like(block_state))
    carried = prefix((block_gate, block_state), "seq", compose, identity_pair)
    incoming = carried[1]
    arriving = []
    arriving.append(incoming)
    arriving = jnp.stack(arriving)
    carry_mask = (stretch_ids == prior_ids[:, None]).astype(jnp.float32)
    carry_decay = jnp.exp(log_decay) * carry_mask[:, :, None]
    from_before = (
        jnp.einsum(
            "cln,chpn->clhp",
            read_state,
            arriving.astype(jnp.bfloat16),
            preferred_element_type=jnp.float32,
        )
        * carry_decay[:, :, :, None]
    )
    result = (
        within_stretch + from_before + skip_gain[None, None, :, None] * values.astype(jnp.float32)
    )
    ssm_rows = result.reshape(block_rows, local_width).astype(jnp.bfloat16)
    end_weight = ends_mask.astype(jnp.float32)
    has_end = jnp.sum(end_weight, axis=1)
    end_decay = jnp.sum(decay_heads * end_weight[:, None, :], axis=2)
    end_ids = jnp.sum(jnp.where(ends_mask, stretch_ids, 0), axis=1)
    keep_end = ((stretch_ids == end_ids[:, None]) & (has_end[:, None] > 0))[:, None, :]
    end_coef = (
        jnp.where(keep_end, jnp.exp(jnp.minimum(end_decay[:, :, None] - decay_heads, 0.0)), 0.0)
        * step_heads
    )
    end_rows = (values.astype(jnp.float32) * jnp.swapaxes(end_coef, 1, 2)[:, :, :, None]).astype(
        jnp.bfloat16
    )
    end_states = jnp.einsum(
        "clhp,cln->chpn", end_rows, write_state, preferred_element_type=jnp.float32
    )
    end_carry = (
        jnp.exp(end_decay) * ((end_ids == prior_ids) & (has_end > 0)).astype(jnp.float32)[:, None]
    )
    end_states = end_states + end_carry[:, :, None, None] * arriving
    final_block = jnp.sum(end_states, axis=0)[None]
    head_gates = gates_sum.astype(jnp.bfloat16)
    norm_slice = lax.dynamic_slice_in_dim(norm_gain, group_index * local_width, local_width)
    gated = ssm_rows.astype(jnp.float32) * jax.nn.silu(head_gates.astype(jnp.float32))
    squares = lax.psum(jnp.sum(gated * gated, axis=1), "head")
    scaled = gated * lax.rsqrt(squares / inner_width + epsilon)[:, None] * norm_slice[None, :]
    outgoing = scaled.astype(jnp.bfloat16)
    returned = lax.all_to_all(
        outgoing.reshape(groups, sub_rows, local_width),
        "head",
        split_axis=0,
        concat_axis=2,
        tiled=True,
    )
    gated_out = returned.reshape(sub_rows, inner_width)
    return (gated_out, final_block)


def solution(mesh):
    in_specs = (
        P(("seq", "head"), None),
        P("seq", "head"),
        P("seq", "head"),
        P("seq", "head"),
        P("seq", None),
        P(),
        P(),
        P("head"),
        P("head"),
        P("head"),
        P(),
        P(),
    )
    out_specs = (P(("seq", "head"), None), P("seq", "head", None, None))
    return jax.shard_map(
        on_device, mesh=mesh, in_specs=in_specs, out_specs=out_specs, check_vma=False
    )
```

profile of v0, /device:TPU:1, one launch (start us, length us, event | category | flops | bytes accessed | tf_op | source)
XLA Modules:
  0.0 279.8 jit_solution(17483713503522964245)
XLA Ops:
  8.0 0.7 all-gather.13.cloned.1.call-update
  9.5 25.8 %all-gather.2 = bf16[8,320,10]{1,2,0:T(8,128)(2,1)S(1)} all-gather(bf16[1,320,10]{1,2,0:T(8,128)(2,1)} %bitcast.152), channel_id=1, replica_groups=mesh['seq'=8,'head'=4] {'seq'}, dimensions={0}, use_global_device_ids=true | all-gather | bytes 57600 | tf_op jit(solution)/shard_map/all_gather | solution.py:77
  40.8 0.8 dynamic_slice.19
  41.6 0.7 select_reduce_fusion
  44.7 1.9 broadcast_multiply_fusion
  48.0 25.1 %all-gather.13.cloned.1.call-done = bf16[2560,256]{1,0:T(8,128)(2,1)} async-done(((bf16[320,256]{1,0:T(8,128)(2,1)}), bf16[2560,256]{1,0:T(8,128)(2,1)}) %all-gather.13.cloned.1.call-update) | async-done | bytes 1310736 | tf_op jit(solution)/shard_map/all_gather | solution.py:76
  73.2 1.8 convolution_convert_fusion.2
  75.0 61.0 %all-gather.11.cloned.1.call-done = bf16[2560,640]{1,0:T(8,128)(2,1)} async-done(((bf16[320,640]{1,0:T(8,128)(2,1)}), bf16[2560,640]{1,0:T(8,128)(2,1)}) %all-gather.11.cloned.1.call-update) | async-done | bytes 3276816 | tf_op jit(solution)/shard_map/all_gather | solution.py:75
  136.0 3.1 %convolution_convert_fusion.1 = bf16[256,640]{1,0:T(8,128)(2,1)S(1)} fusion(bf16[256,2560]{1,0:T(8,128)(2,1)S(1)} %copy-done.1, bf16[2560,640]{1,0:T(8,128)(2,1)} %all-gather.11.cloned.1.call-done), kind=kOutput, calls=%fused_computation.17 | convolution fusion | flops 839024640 | bytes 4915200 | tf_op jit(solution)/shard_map/dot_general | solution.py:72
  139.1 2.2 collective-permute-start
  142.2 0.8 multiply_convert_fusion.10
  143.3 0.9 fusion.14
  145.6 0.8 dynamic_slice.21
  146.7 16.7 %all-gather = bf16[8,10,1]{1,2,0:T(2,128)(2,1)S(1)} all-gather(bf16[1,10,1]{1,2,0:T(2,128)(2,1)S(1)} %get-tuple-element.74), channel_id=2, replica_groups=mesh['seq'=8,'head'=4] {'seq'}, dimensions={0}, use_global_device_ids=true | all-gather | bytes 180 | tf_op jit(solution)/shard_map/all_gather | solution.py:21
  164.3 24.2 %all-gather.17.cloned.1.call-done = bf16[80,64,128]{2,1,0:T(8,128)(2,1)} async-done(((bf16[10,64,128]{2,1,0:T(8,128)(2,1)}), bf16[80,64,128]{2,1,0:T(8,128)(2,1)}) %all-gather.17.cloned.1.call-update) | async-done | bytes 1310736 | tf_op jit(solution)/shard_map/all_gather | solution.py:21
  189.2 1.0 fusion.12
  190.5 60.7 %all-gather.15.cloned.1.call-done = bf16[2560,640]{1,0:T(8,128)(2,1)} async-done(((bf16[320,640]{1,0:T(8,128)(2,1)}), bf16[2560,640]{1,0:T(8,128)(2,1)}) %all-gather.15.cloned.1.call-update) | async-done | bytes 3276816 | tf_op jit(solution)/shard_map/all_gather | solution.py:78
  251.2 3.6 %multiply_reduce_fusion = (f32[256]{0:T(256)S(1)}, f32[256,640]{1,0:T(8,128)S(1)}) fusion(f32[256,640]{1,0:T(8,128)S(1)} %copy.90, bf16[256,2560]{1,0:T(8,128)(2,1)} %all-gather.9.cloned.1.call-done, bf16[2560,640]{1,0:T(8,128)(2,1)} %all-gather.15.cloned.1.call-done), kind=kOutput, calls=%fused_computation.28 | convolution fusion | flops 840335104 | bytes 5899264 | tf_op jit(solution)/shard_map/dot_general | solution.py:72
  254.9 6.6 %psum.7 = f32[256]{0:T(256)S(1)} all-reduce(f32[256]{0:T(256)S(1)} %get-tuple-element.85), channel_id=1, replica_groups=mesh['seq'=8,'head'=4] {'head'}, use_global_device_ids=true, to_apply=%region_9.10 | all-reduce | flops 256 | bytes 2048 | tf_op jit(solution)/shard_map/psum | solution.py:218
  261.4 0.9 multiply_convert_fusion.12
  262.3 4.1 %all-to-all-start = ((bf16[4,64,640]{2,1,0:T(8,128)(2,1)}), bf16[4,64,640]{2,1,0:T(8,128)(2,1)S(1)}, u32[]{:S(2)}, u32[]{:S(2)}) async-start(bf16[4,64,640]{2,1,0:T(8,128)(2,1)} %bitcast.37), calls=%async_computation | async-start | bytes 655360 | tf_op jit(solution)/shard_map/all_to_all | solution.py:221
  266.6 1.0 fusion.13
  267.6 4.7 %all-to-all-done = bf16[4,64,640]{2,1,0:T(8,128)(2,1)S(1)} async-done(((bf16[4,64,640]{2,1,0:T(8,128)(2,1)}), bf16[4,64,640]{2,1,0:T(8,128)(2,1)S(1)}, u32[]{:S(2)}, u32[]{:S(2)}) %all-to-all-start) | async-done | bytes 327712 | tf_op jit(solution)/shard_map/all_to_all | solution.py:221
  272.5 0.8 copy.104
  (94 shorter events, 11.8 us)
Async XLA Ops:
  7.2 28.3 %copy-start.2 = (s32[4]{0:T(128)S(1)}, s32[4]{0:T(128)}, u32[]{:S(2)}) copy-start(s32[4]{0:T(128)} %param.25) | copy-start | bytes 52
  7.2 36.5 %copy-start = (f32[4,2816]{1,0:T(4,128)S(1)}, f32[4,2816]{1,0:T(4,128)}, u32[]{:S(2)}) copy-start(f32[4,2816]{1,0:T(4,128)} %param.19) | copy-start | bytes 135172
  7.2 36.5 %slice-start = ((f32[4,2816]{1,0:T(4,128)}), f32[4,256]{1,0:T(4,128)S(1)}, s32[]{:S(2)}) async-start(f32[4,2816]{1,0:T(4,128)} %param.19), calls=%async_computation.6 | async-start | bytes 8192 | tf_op jit(solution)/shard_map/slice | solution.py:87
  7.2 37.5 %copy-start.3 = (f32[10]{0:T(128)S(1)}, f32[10]{0:T(128)}, u32[]{:S(2)}) copy-start(f32[10]{0:T(128)} %param.22) | copy-start | bytes 124
  7.2 37.5 %copy-start.4 = (f32[10]{0:T(128)S(1)}, f32[10]{0:T(128)}, u32[]{:S(2)}) copy-start(f32[10]{0:T(128)} %param.21) | copy-start | bytes 124
  7.2 37.5 %all-gather.9.cloned.1.call-start = ((), (), s32[]{:S(2)}) async-start(), calls=%async_computation.1 | async-start | bytes 1638400 | tf_op jit(solution)/shard_map/all_gather | solution.py:67
  8.0 65.2 %all-gather.13.cloned.1.call-start = ((), (), s32[]{:S(2)}) async-start(), calls=%async_computation.3 | async-start | bytes 1474560 | tf_op jit(solution)/shard_map/all_gather | solution.py:76
  8.7 127.3 %all-gather.11.cloned.1.call-start = ((), (), s32[]{:S(2)}) async-start(), calls=%async_computation.2 | async-start | bytes 3686400 | tf_op jit(solution)/shard_map/all_gather | solution.py:75
  9.4 179.1 %all-gather.17.cloned.1.call-start = ((), (), s32[]{:S(2)}) async-start(), calls=%async_computation.5 | async-start | bytes 1474560 | tf_op jit(solution)/shard_map/all_gather | solution.py:21
  44.7 28.5 %copy-start.1 = (bf16[256,2560]{1,0:T(8,128)(2,1)S(1)}, bf16[256,2560]{1,0:T(8,128)(2,1)}, u32[]{:S(2)}) copy-start(bf16[256,2560]{1,0:T(8,128)(2,1)} %all-gather.9.cloned.1.call-done) | copy-start | bytes 3932164
  139.1 3.0 %collective-permute-start = (bf16[3,896]{1,0:T(4,128)(2,1)S(1)}, bf16[3,896]{1,0:T(4,128)(2,1)S(1)}, u32[]{:S(2)}, u32[]{:S(2)}) collective-permute-start(bf16[3,896]{1,0:T(4,128)(2,1)S(1)} %fusion.29), channel_id=1, source_target_pairs={{0,4},{4,8},{8,12},{12,16},{16,20},{20,24},{24,28},{1,5},{5,9},{9,... | collective-permute-start | bytes 16136 | tf_op jit(solution)/shard_map/ppermute | solution.py:15
  144.3 107.0 %all-gather.15.cloned.1.call-start = ((), (), s32[]{:S(2)}) async-start(), calls=%async_computation.4 | async-start | bytes 3686400 | tf_op jit(solution)/shard_map/all_gather | solution.py:78
  188.6 0.7 copy-start.5
  262.3 10.0 %all-to-all-start = ((bf16[4,64,640]{2,1,0:T(8,128)(2,1)}), bf16[4,64,640]{2,1,0:T(8,128)(2,1)S(1)}, u32[]{:S(2)}, u32[]{:S(2)}) async-start(bf16[4,64,640]{2,1,0:T(8,128)(2,1)} %bitcast.37), calls=%async_computation | async-start | bytes 655360 | tf_op jit(solution)/shard_map/all_to_all | solution.py:221
Sparse Core Ops, SparseCore 0:
  9.6 20.6 all-gather.8
  32.5 40.6 all-gather.12
  75.3 60.6 all-gather.10
  144.4 44.1 all-gather.16
  190.6 60.6 all-gather.14
where the time goes:
time: 281 us; the launch traced here: 280 us
  waiting for transfers between devices  178 us (63%)
  blocking collectives  49.1 us (17%)
  between operations  18.2 us (6%)
  matrix products  13.8 us (5%)
  local copies, waits for them, and re-layouts  8.05 us (3%)
  starting transfers between devices  6.47 us (2%)
  other arithmetic  5.88 us (2%)
    all_gather x1, waiting for transfers between devices, on_device(): lax.all_gather(w_values, 'seq', axis=0, tiled=True)  61 us
    all_gather x1, waiting for transfers between devices, on_device(): lax.all_gather(w_gates, 'seq', axis=0, tiled=True)  60.7 us
    all_gather x1, blocking collectives, on_device(): lax.all_gather(w_steps, 'seq', axis=0, tiled=True)  25.8 us
    all_gather x1, waiting for transfers between devices, on_device(): lax.all_gather(w_states, 'seq', axis=0, tiled=True)  25.1 us
    all_gather x1, waiting for transfers between devices, prefix(): lax.all_gather(a.astype(kind), axis)  24.2 us
    all_gather x1, blocking collectives, prefix(): lax.all_gather(a.astype(kind), axis)  16.7 us
    dot_general x4, matrix products, contract(): return jnp.dot(block_hidden, piece, preferred_element_type=jnp.float32)  10.5 us
    psum x1, blocking collectives, on_device(): squares = lax.psum(jnp.sum(gated * gated, axis=1), 'head')  6.57 us
  transfers between devices with their start and end apart: 7, of which 5 were waited for; matrix products, arithmetic and copies ran while one was open for 6% of the time, Pallas kernels for 0%

commit v1 on v0

--- a/solution.py
+++ b/solution.py
@@ -1,6 +1,8 @@
 import jax
 import jax.numpy as jnp
 from jax import lax
+from jax.experimental import pallas as pl
+from jax.experimental.pallas import tpu as pltpu
 from jax.sharding import PartitionSpec as P
 
 STRETCH = 256
@@ -38,6 +40,287 @@
 def segments_at(positions, prompt_ends):
     counted = jnp.sum((prompt_ends[None, :] <= positions[:, None]).astype(jnp.int32), axis=1)
     return jnp.where(positions < 0, -1, counted)
+
+
+MESH = pl.DeviceIdType.MESH
+BF16 = jnp.bfloat16
+F32 = jnp.float32
+
+
+def rdma(src, dst, send_sem, recv_sem, seq, head):
+    return pltpu.make_async_remote_copy(
+        src_ref=src,
+        dst_ref=dst,
+        send_sem=send_sem,
+        recv_sem=recv_sem,
+        device_id=(seq, head),
+        device_id_type=MESH,
+    )
+
+
+def project_kernel(
+    hidden_ref,
+    values_ref,
+    small_ref,
+    gates_ref,
+    pre_ref,
+    states_ref,
+    steps_ref,
+    gate_ref,
+    hid,
+    wbuf,
+    out_v,
+    out_s,
+    out_g,
+    in_v,
+    in_s,
+    in_g,
+    own,
+    tile,
+    tiles,
+    local_sem,
+    hid_send,
+    hid_recv,
+    w_send,
+    w_recv,
+    part_send,
+    part_recv,
+    tile_send,
+    tile_recv,
+):
+    s = lax.axis_index("seq")
+    h = lax.axis_index("head")
+    z = lax.div(s, 2)
+    x = lax.rem(s, 2)
+    z_lo = lax.rem(z, 2)
+    z_hi = lax.div(z, 2)
+    beside = s + 1 - 2 * x
+    partner = s + 2 - 4 * z_lo
+    far = s + 4 - 8 * z_hi
+    heads = [lax.rem(h + d, 4) for d in (1, 2, 3)]
+    rows_w = values_ref.shape[0]
+    rows_h = hidden_ref.shape[0]
+    depth = 2 * rows_w
+    width = values_ref.shape[1]
+    narrow = small_ref.shape[1]
+
+    barrier = pltpu.get_barrier_semaphore()
+    for to in (beside, partner, far):
+        pl.semaphore_signal(barrier, inc=1, device_id=(to, h), device_id_type=MESH)
+    for to in heads:
+        pl.semaphore_signal(barrier, inc=1, device_id=(s, to), device_id_type=MESH)
+
+    my_rows = pl.ds(pl.multiple_of(x * rows_w, 64), rows_w)
+    my_tokens = pl.ds(pl.multiple_of(h * rows_h, 64), rows_h)
+    windows = (pl.ds(0, width), pl.ds(width, narrow), pl.ds(width + narrow, width))
+    sources = (values_ref, small_ref, gates_ref)
+
+    def columns(low, zh):
+        return pl.ds(pl.multiple_of((low + 2 * zh) * depth, 128), depth)
+
+    local = []
+    for p in range(3):
+        local.append(
+            pltpu.make_async_copy(
+                sources[p], wbuf.at[z_hi, my_rows, windows[p]], local_sem.at[p]
+            )
+        )
+    for zh in range(2):
+        local.append(
+            pltpu.make_async_copy(
+                hidden_ref.at[:, columns(z_lo, zh)],
+                hid.at[0, zh, my_tokens],
+                local_sem.at[3 + zh],
+            )
+        )
+    for c in local:
+        c.start()
+    pl.semaphore_wait(barrier, 6)
+
+    to_far = [
+        rdma(sources[p], wbuf.at[z_hi, my_rows, windows[p]], w_send.at[0, p], w_recv.at[0, p], far, h)
+        for p in range(3)
+    ]
+    to_beside = [
+        rdma(sources[p], wbuf.at[z_hi, my_rows, windows[p]], w_send.at[1, p], w_recv.at[1, p], beside, h)
+        for p in range(3)
+    ]
+    passed = [
+        rdma(
+            wbuf.at[1 - z_hi, my_rows, windows[p]],
+            wbuf.at[1 - z_hi, my_rows, windows[p]],
+            w_send.at[2, p],
+            w_recv.at[2, p],
+            beside,
+            h,
+        )
+        for p in range(3)
+    ]
+    hid_over = [
+        rdma(
+            hidden_ref.at[:, columns(1 - z_lo, zh)],
+            hid.at[1, zh, my_tokens],
+            hid_send.at[0, zh],
+            hid_recv.at[0, zh],
+            partner,
+            h,
+        )
+        for zh in range(2)
+    ]
+    hid_own = [
+        rdma(
+            hidden_ref.at[:, columns(z_lo, zh)],
+            hid.at[0, zh, my_tokens],
+            hid_send.at[1 + d, zh],
+            hid_recv.at[1 + d, zh],
+            s,
+            heads[d],
+        )
+        for zh in range(2)
+        for d in range(3)
+    ]
+    hid_pass = [
+        rdma(
+            hid.at[1, zh, my_tokens],
+            hid.at[1, zh, my_tokens],
+            hid_send.at[4 + d, zh],
+            hid_recv.at[4 + d, zh],
+            s,
+            heads[d],
+        )
+        for zh in range(2)
+        for d in range(3)
+    ]
+    for c in hid_over:
+        c.start()
+    for p in (0, 1):
+        to_far[p].start()
+    for p in (0, 1):
+        to_beside[p].start()
+    for c in hid_own:
+        c.start()
+    for zh in range(2):
+        hid_over[zh].wait_recv()
+        for d in range(3):
+            hid_pass[3 * zh + d].start()
+    for p in (0, 1):
+        to_far[p].wait_recv()
+        passed[p].start()
+    to_far[2].start()
+    to_beside[2].start()
+    for c in local:
+        c.wait()
+    for c in hid_own:
+        c.wait_recv()
+    for c in hid_pass:
+        c.wait_recv()
+    for p in (0, 1):
+        to_beside[p].wait_recv()
+        passed[p].wait_recv()
+
+    def product(which, window):
+        return jnp.dot(
+            hid[which, 0], wbuf[0, :, window], preferred_element_type=F32
+        ) + jnp.dot(hid[which, 1], wbuf[1, :, window], preferred_element_type=F32)
+
+    out_s[...] = product(1, windows[1])
+    part_s = rdma(out_s, in_s, part_send.at[0], part_recv.at[0], partner, h)
+    part_s.start()
+    out_v[...] = product(1, windows[0]).astype(BF16)
+    part_v = rdma(out_v, in_v, part_send.at[1], part_recv.at[1], partner, h)
+    part_v.start()
+    small = product(0, windows[1])
+    part_s.wait_recv()
+    small = small + in_s[...]
+    steps_ref[...] = small
+    tile[...] = small.astype(BF16)
+    tiles_out = [
+        rdma(tile, tiles.at[h], tile_send.at[d], tile_recv.at[d], s, heads[d]) for d in range(3)
+    ]
+    for c in tiles_out:
+        c.start()
+    tiles[h] = tile[...]
+    own[...] = product(0, windows[0])
+    part_v.wait_recv()
+    pre_ref[...] = (own[...] + in_v[...].astype(F32)).astype(BF16)
+    for c in tiles_out:
+        c.wait_recv()
+    lane = lax.broadcasted_iota(jnp.int32, tile.shape, 1)
+    for half in range(2):
+        first = tiles[2 * half].astype(F32)
+        second = pltpu.roll(tiles[2 * half + 1].astype(F32), narrow // 2, 1)
+        states_ref[:, half * narrow : (half + 1) * narrow] = jnp.where(
+            lane < narrow // 2, first, second
+        ).astype(BF16)
+
+    to_far[2].wait_recv()
+    passed[2].start()
+    to_beside[2].wait_recv()
+    passed[2].wait_recv()
+    out_g[...] = product(1, windows[2]).astype(BF16)
+    part_g = rdma(out_g, in_g, part_send.at[2], part_recv.at[2], partner, h)
+    part_g.start()
+    own[...] = product(0, windows[2])
+    part_g.wait_recv()
+    gate_ref[...] = (own[...] + in_g[...].astype(F32)).astype(BF16)
+    for c in [*to_far, *to_beside, *passed, *hid_over, *hid_own, *hid_pass, *tiles_out]:
+        c.wait_send()
+    for c in (part_s, part_v, part_g):
+        c.wait_send()
+
+
+def project(hidden, w_values, w_gates, w_steps, w_states):
+    group = lax.axis_index("head")
+    rows = hidden.shape[0] * 4
+    width = w_values.shape[1]
+    share = w_states.shape[1] // 4
+    narrow = 2 * share
+    part = lax.dynamic_slice_in_dim(w_states, group * share, share, 1)
+    small = jnp.concatenate(
+        [part, w_steps, jnp.zeros((w_steps.shape[0], narrow - share - w_steps.shape[1]), BF16)],
+        axis=1,
+    )
+    depth = 2 * w_values.shape[0]
+    vmem = pl.BlockSpec(memory_space=pltpu.VMEM)
+    anywhere = pl.BlockSpec(memory_space=pl.ANY)
+    dma = pltpu.SemaphoreType.DMA
+    pre, states, steps, gates = pl.pallas_call(
+        project_kernel,
+        out_shape=(
+            jax.ShapeDtypeStruct((rows, width), BF16),
+            jax.ShapeDtypeStruct((rows, 2 * narrow), BF16),
+            jax.ShapeDtypeStruct((rows, narrow), F32),
+            jax.ShapeDtypeStruct((rows, width), BF16),
+        ),
+        in_specs=[anywhere] * 4,
+        out_specs=[vmem] * 4,
+        scratch_shapes=[
+            pltpu.VMEM((2, 2, rows, depth), BF16),
+            pltpu.VMEM((2, depth, 2 * width + narrow), BF16),
+            pltpu.VMEM((rows, width), BF16),
+            pltpu.VMEM((rows, narrow), F32),
+            pltpu.VMEM((rows, width), BF16),
+            pltpu.VMEM((rows, width), BF16),
+            pltpu.VMEM((rows, narrow), F32),
+            pltpu.VMEM((rows, width), BF16),
+            pltpu.VMEM((rows, width), F32),
+            pltpu.VMEM((rows, narrow), BF16),
+            pltpu.VMEM((4, rows, narrow), BF16),
+            dma((5,)),
+            dma((7, 2)),
+            dma((7, 2)),
+            dma((3, 3)),
+            dma((3, 3)),
+            dma((3,)),
+            dma((3,)),
+            dma((3,)),
+            dma((3,)),
+        ],
+        compiler_params=pltpu.CompilerParams(
+            collective_id=0, has_side_effects=True, vmem_limit_bytes=48 * 1024 * 1024
+        ),
+    )(hidden, w_values, small, w_gates)
+    return pre, states, steps[:, share : share + w_steps.shape[1]], gates
 
 
 def on_device(
@@ -64,23 +347,27 @@
     state_width = w_states.shape[1] // 2
     conv_taps = conv_weight.shape[0]
     prompt_ends = jnp.cumsum(lengths)
-    block_hidden = lax.all_gather(hidden, "head", axis=0, tiled=True)
-    block_rows = block_hidden.shape[0]
-    sub_rows = block_rows // groups
-
-    def contract(piece):
-        return jnp.dot(block_hidden, piece, preferred_element_type=jnp.float32)
-
-    pieces = (
-        lax.all_gather(w_values, "seq", axis=0, tiled=True),
-        lax.all_gather(w_states, "seq", axis=0, tiled=True),
-        lax.all_gather(w_steps, "seq", axis=0, tiled=True),
-        lax.all_gather(w_gates, "seq", axis=0, tiled=True),
-    )
-    values_sum, states_sum, steps_sum, gates_sum = tuple((contract(piece) for piece in pieces))
-    pre_rows = jnp.concatenate(
-        [values_sum.astype(jnp.bfloat16), states_sum.astype(jnp.bfloat16)], axis=1
-    )
+    block_rows = hidden.shape[0] * groups
+    sub_rows = hidden.shape[0]
+    if lax.axis_size("seq") == 8 and groups == 4:
+        values_in, states_in, steps_sum, head_gates = project(
+            hidden, w_values, w_gates, w_steps, w_states
+        )
+    else:
+        block_hidden = lax.all_gather(hidden, "head", axis=0, tiled=True)
+
+        def contract(piece):
+            return jnp.dot(
+                block_hidden,
+                lax.all_gather(piece, "seq", axis=0, tiled=True),
+                preferred_element_type=jnp.float32,
+            )
+
+        values_in = contract(w_values).astype(jnp.bfloat16)
+        states_in = contract(w_states).astype(jnp.bfloat16)
+        steps_sum = contract(w_steps)
+        head_gates = contract(w_gates).astype(jnp.bfloat16)
+    pre_rows = jnp.concatenate([values_in, states_in], axis=1)
     local_taps = jnp.concatenate(
         [
             lax.dynamic_slice_in_dim(conv_weight, group_index * local_width, local_width, 1),
@@ -212,7 +499,6 @@
     )
     end_states = end_states + end_carry[:, :, None, None] * arriving
     final_block = jnp.sum(end_states, axis=0)[None]
-    head_gates = gates_sum.astype(jnp.bfloat16)
     norm_slice = lax.dynamic_slice_in_dim(norm_gain, group_index * local_width, local_width)
     gated = ssm_rows.astype(jnp.float32) * jax.nn.silu(head_gates.astype(jnp.float32))
     squares = lax.psum(jnp.sum(gated * gated, axis=1), "head")

time: 281 us -> 172 us (0.61)
  the two profiles are of different devices: /device:TPU:1 before, /device:TPU:26 now
where the time goes in v1:
time: 172 us
  Pallas kernels  66.6 us (39%)
  waiting for transfers between devices  27 us (16%)
  blocking collectives  22.6 us (13%)
  between operations  18.3 us (11%)
  other arithmetic  16.8 us (10%)
  local copies, waits for them, and re-layouts  12.1 us (7%)
  starting transfers between devices  4.78 us (3%)
  matrix products  3.3 us (2%)
    pallas_call x1, Pallas kernels, project(): pl.pallas_call(project_kernel, out_shape=(jax.ShapeDtypeStruct((rows, wid...  66.6 us
    all_gather x1, waiting for transfers between devices, prefix(): lax.all_gather(a.astype(kind), axis)  21.5 us
    all_gather x1, blocking collectives, prefix(): lax.all_gather(a.astype(kind), axis)  16.8 us
    add x7, other arithmetic, compose(): later[0][:, None, None] * earlier[1] + later[1]  7.3 us
    psum x1, blocking collectives, on_device(): squares = lax.psum(jnp.sum(gated * gated, axis=1), 'head')  5.79 us
    all_to_all x1, waiting for transfers between devices, on_device(): lax.all_to_all(outgoing.reshape(groups, sub_rows, local_width), 'head', s...  5.52 us
    unnamed x34, local copies, waits for them, and re-layouts  4.98 us
    all_to_all x1, starting transfers between devices, on_device(): lax.all_to_all(outgoing.reshape(groups, sub_rows, local_width), 'head', s...  3.45 us
  transfers between devices with their start and end apart: 3, of which 2 were waited for; matrix products, arithmetic and copies ran while one was open for 8% of the time, Pallas kernels for 0%

profile of v1, /device:TPU:26, one launch (start us, length us, event | category | flops | bytes accessed | tf_op | source)
XLA Modules:
  0.0 171.7 jit_solution(17873705917629774506)
XLA Ops:
  7.2 0.9 copy.77
  8.4 1.0 copy-done.1
  9.4 1.0 copy-done.2
  10.4 1.0 copy-done.3
  11.4 66.6 %shard_map.131 = (bf16[256,640]{1,0:T(8,128)(2,1)S(1)}, bf16[256,256]{1,0:T(8,128)(2,1)S(1)}, f32[256,128]{1,0:T(8,128)S(1)}, bf16[256,640]{1,0:T(8,128)(2,1)S(1)}) custom-call(bf16[64,2560]{1,0:T(8,128)(2,1)S(1)} %copy-done.3, bf16[320,640]{1,0:T(8,128)(2,1)S(1)} %copy-done.1, bf16[320,128]{1,0:T(8,128)(2,1)S(1)} %maximum_maximum_fusion.small_ref, ...), custom_call_target="tpu_custom_call" | custom-call | tf_op jit(solution)/shard_map/pallas_call | solution.py:287
  78.1 1.3 collective-permute-start
  93.3 1.5 multiply_convert_fusion.10
  95.4 0.9 fusion.13
  97.4 16.8 %all-gather = bf16[8,10,1]{1,2,0:T(2,128)(2,1)S(1)} all-gather(bf16[1,10,1]{1,2,0:T(2,128)(2,1)S(1)} %copy-done.9), channel_id=2, replica_groups=mesh['seq'=8,'head'=4] {'seq'}, dimensions={0}, use_global_device_ids=true | all-gather | bytes 180 | tf_op jit(solution)/shard_map/all_gather | solution.py:23
  115.9 21.5 %all-gather.4.cloned.1.call-done = bf16[80,64,128]{2,1,0:T(8,128)(2,1)} async-done(((bf16[10,64,128]{2,1,0:T(8,128)(2,1)}), bf16[80,64,128]{2,1,0:T(8,128)(2,1)}) %all-gather.4.cloned.1.call-update) | async-done | bytes 1310736 | tf_op jit(solution)/shard_map/all_gather | solution.py:23
  137.4 7.6 %while.12 = (s32[]{:T(128)}, f32[10,64,128]{2,1,0:T(8,128)S(1)}, s32[]{:T(128)}, bf16[8,10]{1,0:T(8,128)(2,1)S(1)}, bf16[8,10,64,128]{3,2,1,0:T(8,128)(2,1)}, /*index=5*/s32[]{:T(128)}, s32[]{:T(128)}, s32[]{:T(128)}) while((s32[]{:T(128)}, f32[10,64,128]{2,1,0:T(8,128)S(1)}, s32[]{:T(128)}, bf16[8,10]{1,0:T(8,128)(2,1)S(1)}, ...), condition=%wide.region_7.8_spmd, body=%wide.region_6.7_spmd.sunk | while | flops 245775 | bytes 819435 | solution.py:37
  137.5 1.0 convert_add_fusion.2
  138.6 1.0 convert_add_fusion.2
  139.6 1.0 convert_add_fusion.2
  140.7 1.0 convert_add_fusion.2
  141.8 1.0 convert_add_fusion.2
  142.9 1.0 convert_add_fusion.2
  144.0 1.0 convert_add_fusion.2
  145.3 1.0 fusion.11
  146.9 5.8 %psum.7 = f32[256]{0:T(256)S(1)} all-reduce(f32[256]{0:T(256)S(1)} %multiply_reduce_fusion), channel_id=1, replica_groups=mesh['seq'=8,'head'=4] {'head'}, use_global_device_ids=true, to_apply=%region_9.10 | all-reduce | flops 256 | bytes 2048 | tf_op jit(solution)/shard_map/psum | solution.py:504
  152.7 1.0 multiply_convert_fusion.12
  153.6 3.5 %all-to-all-start = ((bf16[4,64,640]{2,1,0:T(8,128)(2,1)}), bf16[4,64,640]{2,1,0:T(8,128)(2,1)S(1)}, u32[]{:S(2)}, u32[]{:S(2)}) async-start(bf16[4,64,640]{2,1,0:T(8,128)(2,1)} %bitcast.37), calls=%async_computation | async-start | bytes 655360 | tf_op jit(solution)/shard_map/all_to_all | solution.py:507
  157.3 1.0 fusion.12
  158.3 5.5 %all-to-all-done = bf16[4,64,640]{2,1,0:T(8,128)(2,1)S(1)} async-done(((bf16[4,64,640]{2,1,0:T(8,128)(2,1)}), bf16[4,64,640]{2,1,0:T(8,128)(2,1)S(1)}, u32[]{:S(2)}, u32[]{:S(2)}) %all-to-all-start) | async-done | bytes 327712 | tf_op jit(solution)/shard_map/all_to_all | solution.py:507
  (111 shorter events, 15.7 us)
Async XLA Ops:
  7.2 1.1 copy-start
  7.2 130.2 %all-gather.4.cloned.1.call-start = ((), (), s32[]{:S(2)}) async-start(), calls=%async_computation.1 | async-start | bytes 1474560 | tf_op jit(solution)/shard_map/all_gather | solution.py:23
  8.1 71.3 %copy-start.12 = (s32[4]{0:T(128)S(1)}, s32[4]{0:T(128)}, u32[]{:S(2)}) copy-start(s32[4]{0:T(128)} %param.25) | copy-start | bytes 52
  8.1 72.3 %copy-start.6 = (f32[10]{0:T(128)S(1)}, f32[10]{0:T(128)}, u32[]{:S(2)}) copy-start(f32[10]{0:T(128)} %param.21) | copy-start | bytes 124
  8.1 72.3 %copy-start.10 = (f32[10]{0:T(128)S(1)}, f32[10]{0:T(128)}, u32[]{:S(2)}) copy-start(f32[10]{0:T(128)} %param.22) | copy-start | bytes 124
  8.4 1.0 copy-start.1
  9.4 1.0 copy-start.2
  10.4 1.0 copy-start.3
  78.0 13.9 %copy-start.5 = (f32[4,2816]{1,0:T(4,128)S(1)}, f32[4,2816]{1,0:T(4,128)}, u32[]{:S(2)}) copy-start(f32[4,2816]{1,0:T(4,128)} %param.19) | copy-start | bytes 135172
  78.1 15.3 %collective-permute-start = (bf16[3,896]{1,0:T(4,128)(2,1)S(1)}, bf16[3,896]{1,0:T(4,128)(2,1)S(1)}, u32[]{:S(2)}, u32[]{:S(2)}) collective-permute-start(bf16[3,896]{1,0:T(4,128)(2,1)S(1)} %slice.99), channel_id=1, source_target_pairs={{0,4},{4,8},{8,12},{12,16},{16,20},{20,24},{24,28},{1,5},{5,9},{9,... | collective-permute-start | bytes 16136 | tf_op jit(solution)/shard_map/ppermute | solution.py:17
  87.8 1.9 %copy-start.7 = (f32[10]{0:T(128)}, f32[10]{0:T(128)S(1)}, u32[]{:S(2)}) copy-start(f32[10]{0:T(128)S(1)} %multiply_reduce_fusion.1) | copy-start | bytes 124
  92.6 0.7 slice-start
  94.8 0.6 copy-start.11
  94.8 2.2 %copy-start.4 = (f32[10,256]{0,1:T(8,128)S(1)}, f32[10,256]{0,1:T(8,128)}, u32[]{:S(2)}) copy-start(f32[10,256]{0,1:T(8,128)} %get-tuple-element.81) | copy-start | bytes 30724
  95.0 2.4 %copy-start.9 = (bf16[1,10,1]{1,2,0:T(2,128)(2,1)S(1)}, bf16[1,10,1]{1,2,0:T(2,128)(2,1)}, u32[]{:S(2)}) copy-start(bf16[1,10,1]{1,2,0:T(2,128)(2,1)} %get-tuple-element.84) | copy-start | bytes 64
  137.4 7.8 %copy-start.13 = (f32[10]{0:T(128)S(1)}, f32[10]{0:T(128)}, u32[]{:S(2)}) copy-start(f32[10]{0:T(128)} %param.23) | copy-start | bytes 124
  146.6 10.5 %copy-start.8 = (f32[10]{0:T(128)S(1)}, f32[10]{0:T(128)}, u32[]{:S(2)}) copy-start(f32[10]{0:T(128)} %copy-done.7) | copy-start | bytes 124
  153.6 10.2 %all-to-all-start = ((bf16[4,64,640]{2,1,0:T(8,128)(2,1)}), bf16[4,64,640]{2,1,0:T(8,128)(2,1)S(1)}, u32[]{:S(2)}, u32[]{:S(2)}) async-start(bf16[4,64,640]{2,1,0:T(8,128)(2,1)} %bitcast.37), calls=%async_computation | async-start | bytes 655360 | tf_op jit(solution)/shard_map/all_to_all | solution.py:507
Sparse Core Ops, SparseCore 0:
  96.5 40.8 all-gather.3

commit v2 on v1

--- a/solution.py
+++ b/solution.py
@@ -58,15 +58,18 @@
     )
 
 
-def project_kernel(
+def layer_kernel(
     hidden_ref,
     values_ref,
     small_ref,
     gates_ref,
-    pre_ref,
-    states_ref,
-    steps_ref,
-    gate_ref,
+    taps_ref,
+    bias_ref,
+    heads_ref,
+    norm_ref,
+    lengths_ref,
+    out_ref,
+    final_ref,
     hid,
     wbuf,
     out_v,
@@ -87,6 +90,29 @@
     part_recv,
     tile_send,
     tile_recv,
+    halo_out,
+    halo_in,
+    ext,
+    conv,
+    cum_ref,
+    cum_rows,
+    dt_rows,
+    carry_ref,
+    end_ref,
+    y_ref,
+    inc,
+    local_out,
+    gate_out,
+    local_in,
+    gate_in,
+    gated,
+    whole,
+    halo_send,
+    halo_recv,
+    state_send,
+    state_recv,
+    turn_send,
+    turn_recv,
 ):
     s = lax.axis_index("seq")
     h = lax.axis_index("head")
@@ -105,8 +131,10 @@
     narrow = small_ref.shape[1]
 
     barrier = pltpu.get_barrier_semaphore()
-    for to in (beside, partner, far):
-        pl.semaphore_signal(barrier, inc=1, device_id=(to, h), device_id_type=MESH)
+    for d in range(1, 8):
+        pl.semaphore_signal(
+            barrier, inc=1, device_id=(lax.rem(s + d, 8), h), device_id_type=MESH
+        )
     for to in heads:
         pl.semaphore_signal(barrier, inc=1, device_id=(s, to), device_id_type=MESH)
 
@@ -135,7 +163,7 @@
         )
     for c in local:
         c.start()
-    pl.semaphore_wait(barrier, 6)
+    pl.semaphore_wait(barrier, 10)
 
     to_far = [
         rdma(sources[p], wbuf.at[z_hi, my_rows, windows[p]], w_send.at[0, p], w_recv.at[0, p], far, h)
@@ -232,7 +260,6 @@
     small = product(0, windows[1])
     part_s.wait_recv()
     small = small + in_s[...]
-    steps_ref[...] = small
     tile[...] = small.astype(BF16)
     tiles_out = [
         rdma(tile, tiles.at[h], tile_send.at[d], tile_recv.at[d], s, heads[d]) for d in range(3)
@@ -241,59 +268,283 @@
         c.start()
     tiles[h] = tile[...]
     own[...] = product(0, windows[0])
+    to_far[2].wait_recv()
+    passed[2].start()
+
+    rows = own.shape[0]
+    start = s * rows
+    count = lengths_ref.shape[0]
+    ends = []
+    for i in range(count):
+        ends.append(lengths_ref[i] + (ends[i - 1] if i else 0))
+
+    def segment(position):
+        found = jnp.where(position < 0, -1, 0)
+        for end in ends:
+            found = found + jnp.where(end <= position, 1, 0)
+        return found
+
+    last_id = segment(start + rows - 1)
+    prior_id = segment(start - 1)
+    end_id = jnp.int32(-2)
+    end_row = jnp.int32(-1)
+    for i, end in enumerate(ends):
+        inside = (end - 1 >= start) & (end - 1 < start + rows)
+        end_id = jnp.where(inside, i, end_id)
+        end_row = jnp.where(inside, end - 1 - start, end_row)
+
+    order = lax.broadcasted_iota(jnp.int32, (rows, rows), 0)
+    across = lax.broadcasted_iota(jnp.int32, (rows, rows), 1)
+    lower = order >= across
+    lower_ones = lower.astype(F32).astype(BF16)
+    lane = lax.broadcasted_iota(jnp.int32, (rows, narrow), 1)
+    token = lax.broadcasted_iota(jnp.int32, (rows, narrow), 0)
+    ids = segment(start + token)
+
+    def parts(value, number):
+        taken = []
+        for _ in range(number):
+            piece = value.astype(BF16)
+            taken.append(piece)
+            value = value - piece.astype(F32)
+        return taken
+
+    share = narrow // 2
+    step = jax.nn.softplus(small + heads_ref[0:1, :])
+    rate = step * heads_ref[1:2, :]
+    cum = jnp.zeros((rows, narrow), F32)
+    for piece in parts(rate, 3):
+        cum = cum - jnp.dot(lower_ones, piece, preferred_element_type=F32)
+    cum_ref[...] = cum
+    cum_rows[...] = cum.T
+    dt_rows[...] = step.T
+    head_row = lax.broadcasted_iota(jnp.int32, (narrow, width), 0) - share
+    channel = lax.broadcasted_iota(jnp.int32, (narrow, width), 1)
+    spread = (
+        ((channel >= head_row * share) & (channel < head_row * share + share))
+        .astype(F32)
+        .astype(BF16)
+    )
+
+    def expand(value, number):
+        total = None
+        for piece in parts(value, number):
+            term = jnp.dot(piece, spread, preferred_element_type=F32)
+            total = term if total is None else total + term
+        return total
+
+    cum_last = cum[rows - 1 : rows, :]
+    cum_end = jnp.sum(jnp.where(token == end_row, cum, 0.0), axis=0, keepdims=True)
+    gate_row = jnp.where(last_id == prior_id, jnp.exp(cum_last), 0.0)
+    end_gate = jnp.where(end_id == prior_id, jnp.exp(cum_end), 0.0)
+    eight = lax.broadcasted_iota(jnp.int32, (8, narrow), 0)
+    rows8 = jnp.where(
+        eight == 0,
+        gate_row,
+        jnp.where(eight == 1, end_gate, jnp.where(eight == 2, heads_ref[2:3, :], 0.0)),
+    )
+    wide8 = expand(rows8, 3)
+    gate_out[...] = wide8
+    tail = jnp.where(ids == last_id, jnp.exp(jnp.minimum(cum_last - cum, 0.0)), 0.0) * step
+    tail_wide = expand(tail, 2)
+    end_ref[...] = expand(
+        jnp.where(ids == end_id, jnp.exp(jnp.minimum(cum_end - cum, 0.0)), 0.0) * step, 2
+    )
+    carry_ref[...] = expand(jnp.where(ids == prior_id, jnp.exp(cum), 0.0), 2)
+
     part_v.wait_recv()
-    pre_ref[...] = (own[...] + in_v[...].astype(F32)).astype(BF16)
+    pre = (own[...] + in_v[...].astype(F32)).astype(BF16)
+    ext[8:, 0:width] = pre.astype(F32)
+    halo_out[:, 0:width] = pre[rows - 16 :, :]
     for c in tiles_out:
         c.wait_recv()
-    lane = lax.broadcasted_iota(jnp.int32, tile.shape, 1)
     for half in range(2):
         first = tiles[2 * half].astype(F32)
-        second = pltpu.roll(tiles[2 * half + 1].astype(F32), narrow // 2, 1)
-        states_ref[:, half * narrow : (half + 1) * narrow] = jnp.where(
-            lane < narrow // 2, first, second
-        ).astype(BF16)
-
-    to_far[2].wait_recv()
-    passed[2].start()
+        second = pltpu.roll(tiles[2 * half + 1].astype(F32), share, 1)
+        both = jnp.where(lane < share, first, second)
+        low = width + half * narrow
+        ext[8:, low : low + narrow] = both
+        halo_out[:, low : low + narrow] = both[rows - 16 :, :].astype(BF16)
+    halo = rdma(
+        halo_out, halo_in, halo_send.at[0], halo_recv.at[0], lax.rem(s + 1, 8), h
+    )
+    halo.start()
+
     to_beside[2].wait_recv()
     passed[2].wait_recv()
     out_g[...] = product(1, windows[2]).astype(BF16)
     part_g = rdma(out_g, in_g, part_send.at[2], part_recv.at[2], partner, h)
     part_g.start()
     own[...] = product(0, windows[2])
+
+    halo.wait_recv()
+    ext[0:8, :] = halo_in[8:16, :].astype(F32)
+    inner = 4 * width
+    same = [
+        (segment(start + token - d) == ids).astype(F32) for d in range(3, 0, -1)
+    ]
+    chunks = (width + 2 * narrow) // narrow
+    for j in range(chunks):
+        low = j * narrow
+        if low < width:
+            from_lane = pl.ds(pl.multiple_of(h * width + low, 128), narrow)
+        else:
+            from_lane = pl.ds(inner + low - width, narrow)
+        taps = taps_ref[:, from_lane]
+        total = jnp.zeros((rows, narrow), F32) + bias_ref[:, from_lane]
+        for tap in range(4):
+            piece = ext[5 + tap : 5 + tap + rows, low : low + narrow] * taps[tap : tap + 1, :]
+            total = total + (piece * same[tap] if tap < 3 else piece)
+        conv[:, low : low + narrow] = jax.nn.silu(total).astype(BF16)
+
+    values = conv[:, 0:width]
+    write_turned = conv[:, width : width + narrow].astype(F32).T.astype(BF16)
+    read_state = conv[:, width + narrow :]
+    local_out[...] = jnp.dot(
+        write_turned,
+        (values.astype(F32) * tail_wide).astype(BF16),
+        preferred_element_type=F32,
+    ).astype(BF16)
+    onward = []
+    for d in range(3):
+        to = lax.rem(s + d + 1, 8)
+        onward.append(
+            (
+                rdma(local_out, local_in.at[d], state_send.at[0, d], state_recv.at[0, d], to, h),
+                rdma(gate_out, gate_in.at[d], state_send.at[1, d], state_recv.at[1, d], to, h),
+            )
+        )
+    for d in range(3):
+
+        @pl.when(s + d + 1 < 8)
+        def _(d=d):
+            onward[d][0].start()
+            onward[d][1].start()
+
+    met = jnp.where(
+        lower & (segment(start + order) == segment(start + across)),
+        jnp.dot(read_state, write_turned, preferred_element_type=F32),
+        0.0,
+    )
+    pairs = width // narrow
+    for j in range(pairs):
+        pair = conv[:, j * narrow : (j + 1) * narrow]
+        halves = []
+        for a in range(2):
+            at = share + 2 * j + a
+            decay = cum_ref[:, at : at + 1] - cum_rows[at : at + 1, :]
+            scores = met * jnp.exp(jnp.minimum(decay, 0.0)) * dt_rows[at : at + 1, :]
+            halves.append(jnp.dot(scores.astype(BF16), pair, preferred_element_type=F32))
+        y_ref[:, j * narrow : (j + 1) * narrow] = jnp.where(lane < share, halves[0], halves[1])
+    end_local = jnp.dot(
+        write_turned,
+        (values.astype(F32) * end_ref[...]).astype(BF16),
+        preferred_element_type=F32,
+    )
+
+    inc[...] = jnp.zeros(inc.shape, F32)
+    for d in range(3):
+
+        @pl.when(s >= d + 1)
+        def _(d=d):
+            onward[d][0].wait_recv()
+            onward[d][1].wait_recv()
+            arrived = local_in[d].astype(F32)
+            for e in range(d):
+                arrived = arrived * gate_in[e, 0:1, :]
+            inc[...] += arrived
+
     part_g.wait_recv()
-    gate_ref[...] = (own[...] + in_g[...].astype(F32)).astype(BF16)
-    for c in [*to_far, *to_beside, *passed, *hid_over, *hid_own, *hid_pass, *tiles_out]:
+    for j in range(pairs):
+        span = slice(j * narrow, (j + 1) * narrow)
+        state = inc[:, span]
+        final_ref[span, :] = (end_local[:, span] + wide8[1:2, span] * state).T
+        before = jnp.dot(read_state, state.astype(BF16), preferred_element_type=F32)
+        y = (
+            y_ref[:, span]
+            + before * carry_ref[:, span]
+            + wide8[2:3, span] * conv[:, span].astype(F32)
+        ).astype(BF16)
+        gate = (own[:, span] + in_g[:, span].astype(F32)).astype(BF16).astype(F32)
+        gated[:, span] = (y.astype(F32) * jax.nn.silu(gate)).astype(BF16)
+
+    my_columns = pl.ds(pl.multiple_of(h * width, 128), width)
+    turned = [
+        rdma(
+            gated.at[pl.ds(pl.multiple_of(heads[d] * rows_h, 64), rows_h)],
+            whole.at[:, my_columns],
+            turn_send.at[d],
+            turn_recv.at[d],
+            s,
+            heads[d],
+        )
+        for d in range(3)
+    ]
+    for c in turned:
+        c.start()
+    keep = pltpu.make_async_copy(gated.at[my_tokens], whole.at[:, my_columns], local_sem.at[5])
+    keep.start()
+    keep.wait()
+    for c in turned:
+        c.wait_recv()
+    full = whole[...].astype(F32)
+    mean = jnp.sum(full * full, axis=1, keepdims=True) / inner
+    out_ref[...] = (full * lax.rsqrt(mean + epsilon) * norm_ref[...]).astype(BF16)
+
+    for c in [*to_far, *to_beside, *passed, *hid_over, *hid_own, *hid_pass, *tiles_out, *turned]:
         c.wait_send()
-    for c in (part_s, part_v, part_g):
+    for c in (part_s, part_v, part_g, halo):
         c.wait_send()
-
-
-def project(hidden, w_values, w_gates, w_steps, w_states):
+    for d in range(3):
+
+        @pl.when(s + d + 1 < 8)
+        def _(d=d):
+            onward[d][0].wait_send()
+            onward[d][1].wait_send()
+
+
+def layer(
+    hidden,
+    w_values,
+    w_gates,
+    w_steps,
+    w_states,
+    conv_weight,
+    conv_bias,
+    step_bias,
+    decay_rate,
+    skip_gain,
+    norm_gain,
+    lengths,
+):
     group = lax.axis_index("head")
     rows = hidden.shape[0] * 4
     width = w_values.shape[1]
+    count = step_bias.shape[0]
     share = w_states.shape[1] // 4
     narrow = 2 * share
     part = lax.dynamic_slice_in_dim(w_states, group * share, share, 1)
     small = jnp.concatenate(
-        [part, w_steps, jnp.zeros((w_steps.shape[0], narrow - share - w_steps.shape[1]), BF16)],
+        [part, w_steps, jnp.zeros((w_steps.shape[0], narrow - share - count), BF16)],
         axis=1,
     )
+    per_head = jnp.pad(
+        jnp.stack([step_bias, decay_rate, skip_gain]), ((0, 5), (share, narrow - share - count))
+    )
     depth = 2 * w_values.shape[0]
+    channels = width + 2 * narrow
     vmem = pl.BlockSpec(memory_space=pltpu.VMEM)
+    smem = pl.BlockSpec(memory_space=pltpu.SMEM)
     anywhere = pl.BlockSpec(memory_space=pl.ANY)
     dma = pltpu.SemaphoreType.DMA
-    pre, states, steps, gates = pl.pallas_call(
-        project_kernel,
+    gated_out, final = pl.pallas_call(
+        layer_kernel,
         out_shape=(
-            jax.ShapeDtypeStruct((rows, width), BF16),
-            jax.ShapeDtypeStruct((rows, 2 * narrow), BF16),
-            jax.ShapeDtypeStruct((rows, narrow), F32),
-            jax.ShapeDtypeStruct((rows, width), BF16),
+            jax.ShapeDtypeStruct(hidden.shape, BF16),
+            jax.ShapeDtypeStruct((width, narrow), F32),
         ),
-        in_specs=[anywhere] * 4,
-        out_specs=[vmem] * 4,
+        in_specs=[anywhere] * 4 + [vmem] * 4 + [smem],
+        out_specs=[vmem] * 2,
         scratch_shapes=[
             pltpu.VMEM((2, 2, rows, depth), BF16),
             pltpu.VMEM((2, depth, 2 * width + narrow), BF16),
@@ -306,7 +557,7 @@
             pltpu.VMEM((rows, width), F32),
             pltpu.VMEM((rows, narrow), BF16),
             pltpu.VMEM((4, rows, narrow), BF16),
-            dma((5,)),
+            dma((6,)),
             dma((7, 2)),
             dma((7, 2)),
             dma((3, 3)),
@@ -315,12 +566,45 @@
             dma((3,)),
             dma((3,)),
             dma((3,)),
+            pltpu.VMEM((16, channels), BF16),
+            pltpu.VMEM((16, channels), BF16),
+            pltpu.VMEM((8 + rows, channels), F32),
+            pltpu.VMEM((rows, channels), BF16),
+            pltpu.VMEM((rows, narrow), F32),
+            pltpu.VMEM((narrow, rows), F32),
+            pltpu.VMEM((narrow, rows), F32),
+            pltpu.VMEM((rows, width), F32),
+            pltpu.VMEM((rows, width), F32),
+            pltpu.VMEM((rows, width), F32),
+            pltpu.VMEM((narrow, width), F32),
+            pltpu.VMEM((narrow, width), BF16),
+            pltpu.VMEM((8, width), F32),
+            pltpu.VMEM((3, narrow, width), BF16),
+            pltpu.VMEM((3, 8, width), F32),
+            pltpu.VMEM((rows, width), BF16),
+            pltpu.VMEM(hidden.shape, BF16),
+            dma((1,)),
+            dma((1,)),
+            dma((2, 3)),
+            dma((2, 3)),
+            dma((3,)),
+            dma((3,)),
         ],
         compiler_params=pltpu.CompilerParams(
             collective_id=0, has_side_effects=True, vmem_limit_bytes=48 * 1024 * 1024
         ),
-    )(hidden, w_values, small, w_gates)
-    return pre, states, steps[:, share : share + w_steps.shape[1]], gates
+    )(
+        hidden,
+        w_values,
+        small,
+        w_gates,
+        conv_weight,
+        conv_bias[None, :],
+        per_head,
+        norm_gain[None, :],
+        lengths,
+    )
+    return gated_out, final.reshape(1, count, width // count, narrow)
 
 
 def on_device(
@@ -338,6 +622,21 @@
     lengths,
 ):
     groups = lax.axis_size("head")
+    if lax.axis_size("seq") == 8 and groups == 4:
+        return layer(
+            hidden,
+            w_values,
+            w_gates,
+            w_steps,
+            w_states,
+            conv_weight,
+            conv_bias,
+            step_bias,
+            decay_rate,
+            skip_gain,
+            norm_gain,
+            lengths,
+        )
     group_index = lax.axis_index("head")
     block_index = lax.axis_index("seq")
     local_width = w_values.shape[1]
@@ -347,27 +646,23 @@
     state_width = w_states.shape[1] // 2
     conv_taps = conv_weight.shape[0]
     prompt_ends = jnp.cumsum(lengths)
-    block_rows = hidden.shape[0] * groups
-    sub_rows = hidden.shape[0]
-    if lax.axis_size("seq") == 8 and groups == 4:
-        values_in, states_in, steps_sum, head_gates = project(
-            hidden, w_values, w_gates, w_steps, w_states
-        )
-    else:
-        block_hidden = lax.all_gather(hidden, "head", axis=0, tiled=True)
-
-        def contract(piece):
-            return jnp.dot(
-                block_hidden,
-                lax.all_gather(piece, "seq", axis=0, tiled=True),
-                preferred_element_type=jnp.float32,
-            )
-
-        values_in = contract(w_values).astype(jnp.bfloat16)
-        states_in = contract(w_states).astype(jnp.bfloat16)
-        steps_sum = contract(w_steps)
-        head_gates = contract(w_gates).astype(jnp.bfloat16)
-    pre_rows = jnp.concatenate([values_in, states_in], axis=1)
+    block_hidden = lax.all_gather(hidden, "head", axis=0, tiled=True)
+    block_rows = block_hidden.shape[0]
+    sub_rows = block_rows // groups
+
+    def contract(piece):
+        return jnp.dot(block_hidden, piece, preferred_element_type=jnp.float32)
+
+    pieces = (
+        lax.all_gather(w_values, "seq", axis=0, tiled=True),
+        lax.all_gather(w_states, "seq", axis=0, tiled=True),
+        lax.all_gather(w_steps, "seq", axis=0, tiled=True),
+        lax.all_gather(w_gates, "seq", axis=0, tiled=True),
+    )
+    values_sum, states_sum, steps_sum, gates_sum = tuple((contract(piece) for piece in pieces))
+    pre_rows = jnp.concatenate(
+        [values_sum.astype(jnp.bfloat16), states_sum.astype(jnp.bfloat16)], axis=1
+    )
     local_taps = jnp.concatenate(
         [
             lax.dynamic_slice_in_dim(conv_weight, group_index * local_width, local_width, 1),
@@ -499,6 +794,7 @@
     )
     end_states = end_states + end_carry[:, :, None, None] * arriving
     final_block = jnp.sum(end_states, axis=0)[None]
+    head_gates = gates_sum.astype(jnp.bfloat16)
     norm_slice = lax.dynamic_slice_in_dim(norm_gain, group_index * local_width, local_width)
     gated = ssm_rows.astype(jnp.float32) * jax.nn.silu(head_gates.astype(jnp.float32))
     squares = lax.psum(jnp.sum(gated * gated, axis=1), "head")

time: 172 us -> 88.2 us (0.51)
  the two profiles are of different devices: /device:TPU:26 before, /device:TPU:17 now
where the time goes in v2:
time: 88.2 us; the launch traced here: 87.8 us
  Pallas kernels  80.3 us (91%)
  local copies, waits for them, and re-layouts  5.86 us (7%)
  other arithmetic  0.93 us (1%)
    pallas_call x1, Pallas kernels, layer(): pl.pallas_call(layer_kernel, out_shape=(jax.ShapeDtypeStruct(hidden.shape...  80.3 us
    unnamed x17, local copies, waits for them, and re-layouts  4.95 us

profile of v2, /device:TPU:17, one launch (start us, length us, event | category | flops | bytes accessed | tf_op | source)
XLA Modules:
  0.0 87.8 jit_solution(6796444694387915710)
XLA Ops:
  0.6 0.0 copy-start
  0.6 0.0 copy-start.6
  0.7 0.0 copy-start.1
  0.7 0.1 pad.10.clone
  0.8 0.8 select_maximum_fusion.heads_ref
  1.6 0.0 copy-done.6
  1.6 0.7 broadcast_in_dim.10.bias_ref
  2.3 0.0 copy-done
  2.3 0.1 constant_dynamic-slice_fusion
  2.4 0.8 copy.14
  3.3 0.0 copy-start.4
  3.3 0.0 copy-start.5
  3.3 0.1 maximum_maximum_fusion.small_ref
  3.4 0.0 copy-done.1
  3.4 0.7 copy-done.4
  4.1 0.0 copy-done.5
  4.1 0.0 copy-start.2
  4.1 1.0 %copy-done.2 = bf16[320,640]{1,0:T(8,128)(2,1)S(1)} copy-done((bf16[320,640]{1,0:T(8,128)(2,1)S(1)}, bf16[320,640]{1,0:T(8,128)(2,1)}, u32[]{:S(2)}) %copy-start.2) | copy-done | bytes 409624
  5.1 0.0 copy-start.3
  5.1 1.0 %copy-done.3 = bf16[64,2560]{1,0:T(8,128)(2,1)S(1)} copy-done((bf16[64,2560]{1,0:T(8,128)(2,1)S(1)}, bf16[64,2560]{1,0:T(8,128)(2,1)}, u32[]{:S(2)}) %copy-start.3) | copy-done | bytes 327704
  6.1 80.3 %shard_map.131 = (bf16[64,2560]{1,0:T(8,128)(2,1)S(1)}, f32[640,128]{1,0:T(8,128)S(1)}) custom-call(bf16[64,2560]{1,0:T(8,128)(2,1)S(1)} %copy-done.3, bf16[320,640]{1,0:T(8,128)(2,1)S(1)} %copy-done.1, bf16[320,128]{1,0:T(8,128)(2,1)S(1)} %maximum_maximum_fusion.small_ref, bf16[320,640]{1,0:T(8,128)(2,1)S(1)} %copy-done.2, f32[4,2816]{1,0:T(4,128)S(1)} %copy-done.4, ...), custom_call_target="tpu_custom_call" | custom-call | tf_op jit(solution)/shard_map/pallas_call | solution.py:540
  86.4 0.7 copy.17
  87.1 0.7 copy.18
  (2 shorter events, 0.0 us)
Async XLA Ops:
  0.6 1.7 %copy-start = (bf16[320,256]{1,0:T(8,128)(2,1)S(1)}, bf16[320,256]{1,0:T(8,128)(2,1)}, u32[]{:S(2)}) copy-start(bf16[320,256]{1,0:T(8,128)(2,1)} %param.16) | copy-start | bytes 491524
  0.6 0.9 %copy-start.6 = (f32[2560]{0:T(1024)S(1)}, f32[2560]{0:T(1024)}, u32[]{:S(2)}) copy-start(f32[2560]{0:T(1024)} %param.22) | copy-start | bytes 30724
  0.7 2.8 %copy-start.1 = (bf16[320,640]{1,0:T(8,128)(2,1)S(1)}, bf16[320,640]{1,0:T(8,128)(2,1)}, u32[]{:S(2)}) copy-start(bf16[320,640]{1,0:T(8,128)(2,1)} %values_ref.1) | copy-start | bytes 1228804
  3.3 0.8 copy-start.4
  3.3 0.8 copy-start.5
  4.1 1.0 %copy-start.2 = (bf16[320,640]{1,0:T(8,128)(2,1)S(1)}, bf16[320,640]{1,0:T(8,128)(2,1)}, u32[]{:S(2)}) copy-start(bf16[320,640]{1,0:T(8,128)(2,1)} %gates_ref.1) | copy-start | bytes 1228804
  5.1 1.0 %copy-start.3 = (bf16[64,2560]{1,0:T(8,128)(2,1)S(1)}, bf16[64,2560]{1,0:T(8,128)(2,1)}, u32[]{:S(2)}) copy-start(bf16[64,2560]{1,0:T(8,128)(2,1)} %hidden_ref.1) | copy-start | bytes 983044

commit v3 on v2

--- a/solution.py
+++ b/solution.py
@@ -140,14 +140,22 @@
 
     my_rows = pl.ds(pl.multiple_of(x * rows_w, 64), rows_w)
     my_tokens = pl.ds(pl.multiple_of(h * rows_h, 64), rows_h)
-    windows = (pl.ds(0, width), pl.ds(width, narrow), pl.ds(width + narrow, width))
-    sources = (values_ref, small_ref, gates_ref)
+    cuts = (0, 2 * narrow, width)
+    gate_cuts = (0, 2 * narrow, 4 * narrow, width)
+    pieces = [(small_ref, 0, width, narrow)]
+    pieces += [(values_ref, a, a, b - a) for a, b in zip(cuts, cuts[1:])]
+    pieces += [
+        (gates_ref, a, width + narrow + a, b - a) for a, b in zip(gate_cuts, gate_cuts[1:])
+    ]
+    sources = [ref.at[:, pl.ds(a, size)] for ref, a, _, size in pieces]
+    windows = [pl.ds(at, size) for _, _, at, size in pieces]
+    number = len(pieces)
 
     def columns(low, zh):
         return pl.ds(pl.multiple_of((low + 2 * zh) * depth, 128), depth)
 
     local = []
-    for p in range(3):
+    for p in range(number):
         local.append(
             pltpu.make_async_copy(
                 sources[p], wbuf.at[z_hi, my_rows, windows[p]], local_sem.at[p]
@@ -158,7 +166,7 @@
             pltpu.make_async_copy(
                 hidden_ref.at[:, columns(z_lo, zh)],
                 hid.at[0, zh, my_tokens],
-                local_sem.at[3 + zh],
+                local_sem.at[number + zh],
             )
         )
     for c in local:
@@ -167,11 +175,11 @@
 
     to_far = [
         rdma(sources[p], wbuf.at[z_hi, my_rows, windows[p]], w_send.at[0, p], w_recv.at[0, p], far, h)
-        for p in range(3)
+        for p in range(number)
     ]
     to_beside = [
         rdma(sources[p], wbuf.at[z_hi, my_rows, windows[p]], w_send.at[1, p], w_recv.at[1, p], beside, h)
-        for p in range(3)
+        for p in range(number)
     ]
     passed = [
         rdma(
@@ -182,7 +190,7 @@
             beside,
             h,
         )
-        for p in range(3)
+        for p in range(number)
     ]
     hid_over = [
         rdma(
@@ -221,9 +229,8 @@
     ]
     for c in hid_over:
         c.start()
-    for p in (0, 1):
+    for p in range(3):
         to_far[p].start()
-    for p in (0, 1):
         to_beside[p].start()
     for c in hid_own:
         c.start()
@@ -231,33 +238,50 @@
         hid_over[zh].wait_recv()
         for d in range(3):
             hid_pass[3 * zh + d].start()
-    for p in (0, 1):
+
+    def forward(p):
         to_far[p].wait_recv()
         passed[p].start()
-    to_far[2].start()
-    to_beside[2].start()
+        if p + 3 < number:
+            to_far[p + 3].start()
+            to_beside[p + 3].start()
+
+    def landed(p):
+        to_beside[p].wait_recv()
+        passed[p].wait_recv()
+
+    def product(which, window):
+        return jnp.dot(
+            hid[which, 0], wbuf[0, :, window], preferred_element_type=F32
+        ) + jnp.dot(hid[which, 1], wbuf[1, :, window], preferred_element_type=F32)
+
+    def span_of(p):
+        _, a, _, size = pieces[p]
+        return slice(a, a + size)
+
+    def to_partner(p, out, arriving):
+        landed(p)
+        span = span_of(p)
+        out[:, span] = product(1, windows[p]).astype(out.dtype)
+        part = rdma(
+            out.at[:, span], arriving.at[:, span], part_send.at[p], part_recv.at[p], partner, h
+        )
+        part.start()
+        return part
+
+    for p in range(3):
+        forward(p)
     for c in local:
         c.wait()
     for c in hid_own:
         c.wait_recv()
     for c in hid_pass:
         c.wait_recv()
-    for p in (0, 1):
-        to_beside[p].wait_recv()
-        passed[p].wait_recv()
-
-    def product(which, window):
-        return jnp.dot(
-            hid[which, 0], wbuf[0, :, window], preferred_element_type=F32
-        ) + jnp.dot(hid[which, 1], wbuf[1, :, window], preferred_element_type=F32)
-
-    out_s[...] = product(1, windows[1])
-    part_s = rdma(out_s, in_s, part_send.at[0], part_recv.at[0], partner, h)
-    part_s.start()
-    out_v[...] = product(1, windows[0]).astype(BF16)
-    part_v = rdma(out_v, in_v, part_send.at[1], part_recv.at[1], partner, h)
-    part_v.start()
-    small = product(0, windows[1])
+    part_s = to_partner(0, out_s, in_s)
+    part_v = [to_partner(1, out_v, in_v)]
+    forward(3)
+    part_v.append(to_partner(2, out_v, in_v))
+    small = product(0, windows[0])
     part_s.wait_recv()
     small = small + in_s[...]
     tile[...] = small.astype(BF16)
@@ -267,9 +291,9 @@
     for c in tiles_out:
         c.start()
     tiles[h] = tile[...]
-    own[...] = product(0, windows[0])
-    to_far[2].wait_recv()
-    passed[2].start()
+    for p in (1, 2):
+        own[:, span_of(p)] = product(0, windows[p])
+    forward(4)
 
     rows = own.shape[0]
     start = s * rows
@@ -352,7 +376,9 @@
     )
     carry_ref[...] = expand(jnp.where(ids == prior_id, jnp.exp(cum), 0.0), 2)
 
-    part_v.wait_recv()
+    forward(5)
+    for c in part_v:
+        c.wait_recv()
     pre = (own[...] + in_v[...].astype(F32)).astype(BF16)
     ext[8:, 0:width] = pre.astype(F32)
     halo_out[:, 0:width] = pre[rows - 16 :, :]
@@ -370,12 +396,8 @@
     )
     halo.start()
 
-    to_beside[2].wait_recv()
-    passed[2].wait_recv()
-    out_g[...] = product(1, windows[2]).astype(BF16)
-    part_g = rdma(out_g, in_g, part_send.at[2], part_recv.at[2], partner, h)
-    part_g.start()
-    own[...] = product(0, windows[2])
+    part_g = [to_partner(3, out_g, in_g)]
+    own[:, span_of(3)] = product(0, windows[3])
 
     halo.wait_recv()
     ext[0:8, :] = halo_in[8:16, :].astype(F32)
@@ -421,6 +443,8 @@
             onward[d][0].start()
             onward[d][1].start()
 
+    part_g.append(to_partner(4, out_g, in_g))
+    own[:, span_of(4)] = product(0, windows[4])
     met = jnp.where(
         lower & (segment(start + order) == segment(start + across)),
         jnp.dot(read_state, write_turned, preferred_element_type=F32),
@@ -442,6 +466,9 @@
         preferred_element_type=F32,
     )
 
+    part_g.append(to_partner(5, out_g, in_g))
+    own[:, span_of(5)] = product(0, windows[5])
+
     inc[...] = jnp.zeros(inc.shape, F32)
     for d in range(3):
 
@@ -454,7 +481,8 @@
                 arrived = arrived * gate_in[e, 0:1, :]
             inc[...] += arrived
 
-    part_g.wait_recv()
+    for c in part_g:
+        c.wait_recv()
     for j in range(pairs):
         span = slice(j * narrow, (j + 1) * narrow)
         state = inc[:, span]
@@ -482,7 +510,7 @@
     ]
     for c in turned:
         c.start()
-    keep = pltpu.make_async_copy(gated.at[my_tokens], whole.at[:, my_columns], local_sem.at[5])
+    keep = pltpu.make_async_copy(gated.at[my_tokens], whole.at[:, my_columns], local_sem.at[number + 2])
     keep.start()
     keep.wait()
     for c in turned:
@@ -493,7 +521,7 @@
 
     for c in [*to_far, *to_beside, *passed, *hid_over, *hid_own, *hid_pass, *tiles_out, *turned]:
         c.wait_send()
-    for c in (part_s, part_v, part_g, halo):
+    for c in [part_s, *part_v, *part_g, halo]:
         c.wait_send()
     for d in range(3):
 
@@ -557,13 +585,13 @@
             pltpu.VMEM((rows, width), F32),
             pltpu.VMEM((rows, narrow), BF16),
             pltpu.VMEM((4, rows, narrow), BF16),
-            dma((6,)),
+            dma((9,)),
             dma((7, 2)),
             dma((7, 2)),
-            dma((3, 3)),
-            dma((3, 3)),
-            dma((3,)),
-            dma((3,)),
+            dma((3, 6)),
+            dma((3, 6)),
+            dma((6,)),
+            dma((6,)),
             dma((3,)),
             dma((3,)),
             pltpu.VMEM((16, channels), BF16),
@@ -591,7 +619,7 @@
             dma((3,)),
         ],
         compiler_params=pltpu.CompilerParams(
-            collective_id=0, has_side_effects=True, vmem_limit_bytes=48 * 1024 * 1024
+            collective_id=0, has_side_effects=True, vmem_limit_bytes=60 * 1024 * 1024
         ),
     )(
         hidden,

time: 88.2 us -> 85.4 us (0.968)
  the two profiles are of different devices: /device:TPU:17 before, /device:TPU:11 now
where the time goes in v3:
time: 85.4 us; the launch traced here: 85 us
  Pallas kernels  77.5 us (91%)
  local copies, waits for them, and re-layouts  5.37 us (6%)
  other arithmetic  1.41 us (2%)
    pallas_call x1, Pallas kernels, layer(): pl.pallas_call(layer_kernel, out_shape=(jax.ShapeDtypeStruct(hidden.shape...  77.5 us
    unnamed x19, local copies, waits for them, and re-layouts  3.99 us

profile of v3, /device:TPU:11, one launch (start us, length us, event | category | flops | bytes accessed | tf_op | source)
XLA Modules:
  0.0 85.0 jit_solution(13202766402247862747)
XLA Ops:
  0.6 0.0 copy-start
  0.6 0.0 copy-start.3
  0.7 0.0 copy-start.5
  0.7 0.0 copy-start.6
  0.7 0.0 copy-start.7
  0.7 0.1 pad.10.clone
  0.8 0.6 copy-done.5
  1.4 0.0 copy-done.6
  1.4 0.0 copy-done.7
  1.4 0.7 select_maximum_fusion.heads_ref
  2.1 0.0 copy-done.3
  2.1 0.6 broadcast_in_dim.11.norm_ref
  2.7 0.1 copy-done.2
  2.8 0.6 broadcast_in_dim.10.bias_ref
  3.4 0.0 copy-done
  3.4 0.1 constant_dynamic-slice_fusion
  3.5 0.6 copy-done.4
  4.1 0.1 copy.14
  4.2 0.7 maximum_maximum_fusion.small_ref
  5.0 77.5 %shard_map.131 = (bf16[64,2560]{1,0:T(8,128)(2,1)}, f32[640,128]{1,0:T(8,128)}) custom-call(bf16[64,2560]{1,0:T(8,128)(2,1)} %hidden_ref.1, bf16[320,640]{1,0:T(8,128)(2,1)} %values_ref.1, bf16[320,128]{1,0:T(8,128)(2,1)} %maximum_maximum_fusion.small_ref, bf16[320,640]{1,0:T(8,128)(2,1)} %gates_ref.1, f32[4,2816]{1,0:T(4,128)} %taps_ref.1, ...), custom_call_target="tpu_custom_call" | custom-call | tf_op jit(solution)/shard_map/pallas_call | solution.py:568
  82.5 0.0 copy-start.1
  82.5 1.8 %copy.17 = bf16[64,2560]{1,0:T(8,128)(2,1)} copy(bf16[64,2560]{1,0:T(8,128)(2,1)} %get-tuple-element.8) | data formatting | bytes 655360
  84.3 0.0 copy-done.1
  84.3 0.7 copy.18
  (3 shorter events, 0.0 us)
Async XLA Ops:
  0.6 2.8 %copy-start = (bf16[320,256]{1,0:T(8,128)(2,1)S(1)}, bf16[320,256]{1,0:T(8,128)(2,1)}, u32[]{:S(2)}) copy-start(bf16[320,256]{1,0:T(8,128)(2,1)} %param.16) | copy-start | bytes 491524
  0.6 1.4 %copy-start.3 = (f32[2560]{0:T(1024)S(1)}, f32[2560]{0:T(1024)}, u32[]{:S(2)}) copy-start(f32[2560]{0:T(1024)} %param.22) | copy-start | bytes 30724
  0.7 0.7 copy-start.5
  0.7 0.7 copy-start.6
  0.7 0.7 copy-start.7
  2.1 0.7 copy-start.2
  3.4 0.7 copy-start.4
  82.5 1.8 %copy-start.1 = (f32[640,128]{1,0:T(8,128)S(1)}, f32[640,128]{1,0:T(8,128)}, u32[]{:S(2)}) copy-start(f32[640,128]{1,0:T(8,128)} %get-tuple-element.5) | copy-start | bytes 983044

commit v4 on v3

--- a/solution.py
+++ b/solution.py
@@ -61,12 +61,13 @@
 def layer_kernel(
     hidden_ref,
     values_ref,
-    small_ref,
     gates_ref,
-    taps_ref,
+    states_ref,
+    steps_ref,
+    channel_ref,
     bias_ref,
-    heads_ref,
-    norm_ref,
+    decay_ref,
+    skip_ref,
     lengths_ref,
     out_ref,
     final_ref,
@@ -113,6 +114,8 @@
     state_recv,
     turn_send,
     turn_recv,
+    small_ref,
+    local_f32,
 ):
     s = lax.axis_index("seq")
     h = lax.axis_index("head")
@@ -129,7 +132,9 @@
     depth = 2 * rows_w
     width = values_ref.shape[1]
     narrow = small_ref.shape[1]
-
+    count_heads = steps_ref.shape[0]
+
+    share = narrow // 2
     barrier = pltpu.get_barrier_semaphore()
     for d in range(1, 8):
         pl.semaphore_signal(
@@ -137,6 +142,26 @@
         )
     for to in heads:
         pl.semaphore_signal(barrier, inc=1, device_id=(s, to), device_id_type=MESH)
+
+    wide_states = states_ref[
+        :, pl.ds(pl.multiple_of(lax.div(h, 2) * narrow, 128), narrow)
+    ].astype(F32)
+    turned_states = pltpu.roll(wide_states, share, 1)
+    place = (
+        lax.broadcasted_iota(jnp.int32, (count_heads, narrow), 1)
+        == lax.broadcasted_iota(jnp.int32, (count_heads, narrow), 0) + share
+    )
+    step_columns = lax.dot_general(
+        steps_ref[...],
+        place.astype(F32).astype(BF16),
+        (((0,), (0,)), ((), ())),
+        preferred_element_type=F32,
+    )
+    small_ref[...] = jnp.where(
+        lax.broadcasted_iota(jnp.int32, small_ref.shape, 1) < share,
+        jnp.where(lax.rem(h, 2) == 1, turned_states, wide_states),
+        step_columns,
+    ).astype(BF16)
 
     my_rows = pl.ds(pl.multiple_of(x * rows_w, 64), rows_w)
     my_tokens = pl.ds(pl.multiple_of(h * rows_h, 64), rows_h)
@@ -283,7 +308,7 @@
     part_v.append(to_partner(2, out_v, in_v))
     small = product(0, windows[0])
     part_s.wait_recv()
-    small = small + in_s[...]
+    small = small + in_s[...].astype(F32)
     tile[...] = small.astype(BF16)
     tiles_out = [
         rdma(tile, tiles.at[h], tile_send.at[d], tile_recv.at[d], s, heads[d]) for d in range(3)
@@ -333,9 +358,16 @@
             value = value - piece.astype(F32)
         return taken
 
-    share = narrow // 2
-    step = jax.nn.softplus(small + heads_ref[0:1, :])
-    rate = step * heads_ref[1:2, :]
+    head_lane = lax.broadcasted_iota(jnp.int32, (8, narrow), 1) - share
+
+    def over_lanes(ref):
+        row = jnp.zeros((8, narrow), F32)
+        for i in range(count_heads):
+            row = jnp.where(head_lane == i, ref[i], row)
+        return row
+
+    step = jax.nn.softplus(small + over_lanes(bias_ref)[0:1, :])
+    rate = step * over_lanes(decay_ref)[0:1, :]
     cum = jnp.zeros((rows, narrow), F32)
     for piece in parts(rate, 3):
         cum = cum - jnp.dot(lower_ones, piece, preferred_element_type=F32)
@@ -365,7 +397,7 @@
     rows8 = jnp.where(
         eight == 0,
         gate_row,
-        jnp.where(eight == 1, end_gate, jnp.where(eight == 2, heads_ref[2:3, :], 0.0)),
+        jnp.where(eight == 1, end_gate, jnp.where(eight == 2, over_lanes(skip_ref), 0.0)),
     )
     wide8 = expand(rows8, 3)
     gate_out[...] = wide8
@@ -412,8 +444,8 @@
             from_lane = pl.ds(pl.multiple_of(h * width + low, 128), narrow)
         else:
             from_lane = pl.ds(inner + low - width, narrow)
-        taps = taps_ref[:, from_lane]
-        total = jnp.zeros((rows, narrow), F32) + bias_ref[:, from_lane]
+        taps = channel_ref[:, from_lane]
+        total = jnp.zeros((rows, narrow), F32) + taps[4:5, :]
         for tap in range(4):
             piece = ext[5 + tap : 5 + tap + rows, low : low + narrow] * taps[tap : tap + 1, :]
             total = total + (piece * same[tap] if tap < 3 else piece)
@@ -422,29 +454,43 @@
     values = conv[:, 0:width]
     write_turned = conv[:, width : width + narrow].astype(F32).T.astype(BF16)
     read_state = conv[:, width + narrow :]
-    local_out[...] = jnp.dot(
+    local = jnp.dot(
         write_turned,
         (values.astype(F32) * tail_wide).astype(BF16),
         preferred_element_type=F32,
-    ).astype(BF16)
-    onward = []
-    for d in range(3):
-        to = lax.rem(s + d + 1, 8)
-        onward.append(
-            (
-                rdma(local_out, local_in.at[d], state_send.at[0, d], state_recv.at[0, d], to, h),
-                rdma(gate_out, gate_in.at[d], state_send.at[1, d], state_recv.at[1, d], to, h),
-            )
-        )
-    for d in range(3):
-
-        @pl.when(s + d + 1 < 8)
-        def _(d=d):
-            onward[d][0].start()
-            onward[d][1].start()
+    )
+    local_f32[...] = local
+    local_out[0] = local.astype(BF16)
+    next_one = (
+        rdma(
+            local_out.at[0], local_in.at[0], state_send.at[0], state_recv.at[0], lax.rem(s + 1, 8), h
+        ),
+        rdma(gate_out, gate_in, state_send.at[1], state_recv.at[1], lax.rem(s + 1, 8), h),
+    )
+    next_two = rdma(
+        local_out.at[1], local_in.at[1], state_send.at[2], state_recv.at[2], lax.rem(s + 2, 8), h
+    )
+
+    @pl.when(s < 7)
+    def _():
+        for c in next_one:
+            c.start()
 
     part_g.append(to_partner(4, out_g, in_g))
     own[:, span_of(4)] = product(0, windows[4])
+    inc[...] = jnp.zeros(inc.shape, F32)
+
+    @pl.when(s > 0)
+    def _():
+        for c in next_one:
+            c.wait_recv()
+        inc[...] = local_in[0].astype(F32)
+
+    @pl.when(s < 6)
+    def _():
+        local_out[1] = (local_f32[...] + wide8[0:1, :] * inc[...]).astype(BF16)
+        next_two.start()
+
     met = jnp.where(
         lower & (segment(start + order) == segment(start + across)),
         jnp.dot(read_state, write_turned, preferred_element_type=F32),
@@ -469,17 +515,10 @@
     part_g.append(to_partner(5, out_g, in_g))
     own[:, span_of(5)] = product(0, windows[5])
 
-    inc[...] = jnp.zeros(inc.shape, F32)
-    for d in range(3):
-
-        @pl.when(s >= d + 1)
-        def _(d=d):
-            onward[d][0].wait_recv()
-            onward[d][1].wait_recv()
-            arrived = local_in[d].astype(F32)
-            for e in range(d):
-                arrived = arrived * gate_in[e, 0:1, :]
-            inc[...] += arrived
+    @pl.when(s > 1)
+    def _():
+        next_two.wait_recv()
+        inc[...] += gate_in[0:1, :] * local_in[1].astype(F32)
 
     for c in part_g:
         c.wait_recv()
@@ -517,18 +556,21 @@
         c.wait_recv()
     full = whole[...].astype(F32)
     mean = jnp.sum(full * full, axis=1, keepdims=True) / inner
-    out_ref[...] = (full * lax.rsqrt(mean + epsilon) * norm_ref[...]).astype(BF16)
+    out_ref[...] = (full * lax.rsqrt(mean + epsilon) * channel_ref[5:6, 0:inner]).astype(BF16)
 
     for c in [*to_far, *to_beside, *passed, *hid_over, *hid_own, *hid_pass, *tiles_out, *turned]:
         c.wait_send()
     for c in [part_s, *part_v, *part_g, halo]:
         c.wait_send()
-    for d in range(3):
-
-        @pl.when(s + d + 1 < 8)
-        def _(d=d):
-            onward[d][0].wait_send()
-            onward[d][1].wait_send()
+
+    @pl.when(s < 7)
+    def _():
+        for c in next_one:
+            c.wait_send()
+
+    @pl.when(s < 6)
+    def _():
+        next_two.wait_send()
 
 
 def layer(
@@ -545,19 +587,19 @@
     norm_gain,
     lengths,
 ):
-    group = lax.axis_index("head")
     rows = hidden.shape[0] * 4
     width = w_values.shape[1]
     count = step_bias.shape[0]
-    share = w_states.shape[1] // 4
-    narrow = 2 * share
-    part = lax.dynamic_slice_in_dim(w_states, group * share, share, 1)
-    small = jnp.concatenate(
-        [part, w_steps, jnp.zeros((w_steps.shape[0], narrow - share - count), BF16)],
-        axis=1,
-    )
-    per_head = jnp.pad(
-        jnp.stack([step_bias, decay_rate, skip_gain]), ((0, 5), (share, narrow - share - count))
+    narrow = w_states.shape[1] // 2
+    inner = norm_gain.shape[0]
+    per_channel = jnp.concatenate(
+        [
+            conv_weight,
+            conv_bias[None, :],
+            jnp.pad(norm_gain, (0, conv_bias.shape[0] - inner))[None, :],
+            jnp.zeros((2, conv_bias.shape[0]), F32),
+        ],
+        axis=0,
     )
     depth = 2 * w_values.shape[0]
     channels = width + 2 * narrow
@@ -571,16 +613,16 @@
             jax.ShapeDtypeStruct(hidden.shape, BF16),
             jax.ShapeDtypeStruct((width, narrow), F32),
         ),
-        in_specs=[anywhere] * 4 + [vmem] * 4 + [smem],
+        in_specs=[anywhere] * 3 + [vmem] * 3 + [smem] * 4,
         out_specs=[vmem] * 2,
         scratch_shapes=[
             pltpu.VMEM((2, 2, rows, depth), BF16),
             pltpu.VMEM((2, depth, 2 * width + narrow), BF16),
             pltpu.VMEM((rows, width), BF16),
-            pltpu.VMEM((rows, narrow), F32),
+            pltpu.VMEM((rows, narrow), BF16),
             pltpu.VMEM((rows, width), BF16),
             pltpu.VMEM((rows, width), BF16),
-            pltpu.VMEM((rows, narrow), F32),
+            pltpu.VMEM((rows, narrow), BF16),
             pltpu.VMEM((rows, width), BF16),
             pltpu.VMEM((rows, width), F32),
             pltpu.VMEM((rows, narrow), BF16),
@@ -605,18 +647,20 @@
             pltpu.VMEM((rows, width), F32),
             pltpu.VMEM((rows, width), F32),
             pltpu.VMEM((narrow, width), F32),
-            pltpu.VMEM((narrow, width), BF16),
+            pltpu.VMEM((2, narrow, width), BF16),
             pltpu.VMEM((8, width), F32),
-            pltpu.VMEM((3, narrow, width), BF16),
-            pltpu.VMEM((3, 8, width), F32),
+            pltpu.VMEM((2, narrow, width), BF16),
+            pltpu.VMEM((8, width), F32),
             pltpu.VMEM((rows, width), BF16),
             pltpu.VMEM(hidden.shape, BF16),
             dma((1,)),
             dma((1,)),
-            dma((2, 3)),
-            dma((2, 3)),
             dma((3,)),
             dma((3,)),
+            dma((3,)),
+            dma((3,)),
+            pltpu.VMEM((w_values.shape[0], narrow), BF16),
+            pltpu.VMEM((narrow, width), F32),
         ],
         compiler_params=pltpu.CompilerParams(
             collective_id=0, has_side_effects=True, vmem_limit_bytes=60 * 1024 * 1024
@@ -624,12 +668,13 @@
     )(
         hidden,
         w_values,
-        small,
         w_gates,
-        conv_weight,
-        conv_bias[None, :],
-        per_head,
-        norm_gain[None, :],
+        w_states,
+        w_steps.T,
+        per_channel,
+        step_bias,
+        decay_rate,
+        skip_gain,
         lengths,
     )
     return gated_out, final.reshape(1, count, width // count, narrow)

time: 85.4 us -> 79.4 us (0.930)
  the two profiles are of different devices: /device:TPU:11 before, /device:TPU:1 now
where the time goes in v4:
time: 79.4 us; the launch traced here: 79.1 us
  Pallas kernels  73.7 us (93%)
  local copies, waits for them, and re-layouts  4.01 us (5%)
    pallas_call x1, Pallas kernels, layer(): pl.pallas_call(layer_kernel, out_shape=(jax.ShapeDtypeStruct(hidden.shape...  73.7 us
    unnamed x6, local copies, waits for them, and re-layouts  2.5 us

profile of v4, /device:TPU:1, one launch (start us, length us, event | category | flops | bytes accessed | tf_op | source)
XLA Modules:
  0.0 79.1 jit_solution(8531843033498258882)
XLA Ops:
  0.6 0.0 copy-start.1
  0.6 0.1 pad.8.clone
  0.7 0.7 broadcast_in_dim.9
  1.4 0.7 pad.4
  2.2 0.0 copy-done.1
  2.2 0.7 maximum_maximum_fusion.channel_ref
  2.9 73.7 %shard_map.131 = (bf16[64,2560]{1,0:T(8,128)(2,1)}, f32[640,128]{1,0:T(8,128)}) custom-call(bf16[64,2560]{1,0:T(8,128)(2,1)} %hidden_ref.1, bf16[320,640]{1,0:T(8,128)(2,1)} %values_ref.1, bf16[320,640]{1,0:T(8,128)(2,1)} %gates_ref.1, bf16[320,256]{1,0:T(8,128)(2,1)} %states_ref.1, bf16[10,320]{1,0:T(8,128)(2,1)} %bitcast.3, ...), custom_call_target="tpu_custom_call" | custom-call | tf_op jit(solution)/shard_map/pallas_call | solution.py:610
  76.6 0.0 copy-start
  76.6 1.8 %copy.16 = bf16[64,2560]{1,0:T(8,128)(2,1)} copy(bf16[64,2560]{1,0:T(8,128)(2,1)} %get-tuple-element.8) | data formatting | bytes 655360
  78.4 0.0 copy-done
  78.4 0.7 copy.17
  (2 shorter events, 0.0 us)
Async XLA Ops:
  0.6 1.5 %copy-start.1 = (f32[4,2816]{1,0:T(4,128)S(1)}, f32[4,2816]{1,0:T(4,128)}, u32[]{:S(2)}) copy-start(f32[4,2816]{1,0:T(4,128)} %param.17) | copy-start | bytes 135172
  76.6 1.8 %copy-start = (f32[640,128]{1,0:T(8,128)S(1)}, f32[640,128]{1,0:T(8,128)}, u32[]{:S(2)}) copy-start(f32[640,128]{1,0:T(8,128)} %get-tuple-element.5) | copy-start | bytes 983044

commit v5 on v4

--- a/solution.py
+++ b/solution.py
@@ -64,7 +64,9 @@
     gates_ref,
     states_ref,
     steps_ref,
-    channel_ref,
+    taps_ref,
+    offset_ref,
+    norm_ref,
     bias_ref,
     decay_ref,
     skip_ref,
@@ -294,8 +296,8 @@
         part.start()
         return part
 
-    for p in range(3):
-        forward(p)
+    forward(0)
+    forward(1)
     for c in local:
         c.wait()
     for c in hid_own:
@@ -303,10 +305,8 @@
     for c in hid_pass:
         c.wait_recv()
     part_s = to_partner(0, out_s, in_s)
+    small = product(0, windows[0])
     part_v = [to_partner(1, out_v, in_v)]
-    forward(3)
-    part_v.append(to_partner(2, out_v, in_v))
-    small = product(0, windows[0])
     part_s.wait_recv()
     small = small + in_s[...].astype(F32)
     tile[...] = small.astype(BF16)
@@ -316,9 +316,7 @@
     for c in tiles_out:
         c.start()
     tiles[h] = tile[...]
-    for p in (1, 2):
-        own[:, span_of(p)] = product(0, windows[p])
-    forward(4)
+    own[:, span_of(1)] = product(0, windows[1])
 
     rows = own.shape[0]
     start = s * rows
@@ -408,12 +406,6 @@
     )
     carry_ref[...] = expand(jnp.where(ids == prior_id, jnp.exp(cum), 0.0), 2)
 
-    forward(5)
-    for c in part_v:
-        c.wait_recv()
-    pre = (own[...] + in_v[...].astype(F32)).astype(BF16)
-    ext[8:, 0:width] = pre.astype(F32)
-    halo_out[:, 0:width] = pre[rows - 16 :, :]
     for c in tiles_out:
         c.wait_recv()
     for half in range(2):
@@ -423,13 +415,18 @@
         low = width + half * narrow
         ext[8:, low : low + narrow] = both
         halo_out[:, low : low + narrow] = both[rows - 16 :, :].astype(BF16)
+    forward(2)
+    part_v.append(to_partner(2, out_v, in_v))
+    own[:, span_of(2)] = product(0, windows[2])
+    for c in part_v:
+        c.wait_recv()
+    pre = (own[...] + in_v[...].astype(F32)).astype(BF16)
+    ext[8:, 0:width] = pre.astype(F32)
+    halo_out[:, 0:width] = pre[rows - 16 :, :]
     halo = rdma(
         halo_out, halo_in, halo_send.at[0], halo_recv.at[0], lax.rem(s + 1, 8), h
     )
     halo.start()
-
-    part_g = [to_partner(3, out_g, in_g)]
-    own[:, span_of(3)] = product(0, windows[3])
 
     halo.wait_recv()
     ext[0:8, :] = halo_in[8:16, :].astype(F32)
@@ -442,10 +439,12 @@
         low = j * narrow
         if low < width:
             from_lane = pl.ds(pl.multiple_of(h * width + low, 128), narrow)
+            offset = offset_ref[pl.ds(h * (width // narrow) + j, 1), :]
         else:
             from_lane = pl.ds(inner + low - width, narrow)
-        taps = channel_ref[:, from_lane]
-        total = jnp.zeros((rows, narrow), F32) + taps[4:5, :]
+            offset = offset_ref[pl.ds((inner + low - width) // narrow, 1), :]
+        taps = taps_ref[:, from_lane]
+        total = jnp.zeros((rows, narrow), F32) + offset
         for tap in range(4):
             piece = ext[5 + tap : 5 + tap + rows, low : low + narrow] * taps[tap : tap + 1, :]
             total = total + (piece * same[tap] if tap < 3 else piece)
@@ -476,8 +475,6 @@
         for c in next_one:
             c.start()
 
-    part_g.append(to_partner(4, out_g, in_g))
-    own[:, span_of(4)] = product(0, windows[4])
     inc[...] = jnp.zeros(inc.shape, F32)
 
     @pl.when(s > 0)
@@ -491,6 +488,7 @@
         local_out[1] = (local_f32[...] + wide8[0:1, :] * inc[...]).astype(BF16)
         next_two.start()
 
+    forward(3)
     met = jnp.where(
         lower & (segment(start + order) == segment(start + across)),
         jnp.dot(read_state, write_turned, preferred_element_type=F32),
@@ -512,51 +510,75 @@
         preferred_element_type=F32,
     )
 
-    part_g.append(to_partner(5, out_g, in_g))
-    own[:, span_of(5)] = product(0, windows[5])
+    part_g = [to_partner(3, out_g, in_g)]
+    own[:, span_of(3)] = product(0, windows[3])
 
     @pl.when(s > 1)
     def _():
         next_two.wait_recv()
         inc[...] += gate_in[0:1, :] * local_in[1].astype(F32)
 
-    for c in part_g:
-        c.wait_recv()
     for j in range(pairs):
         span = slice(j * narrow, (j + 1) * narrow)
         state = inc[:, span]
         final_ref[span, :] = (end_local[:, span] + wide8[1:2, span] * state).T
         before = jnp.dot(read_state, state.astype(BF16), preferred_element_type=F32)
-        y = (
+        y_ref[:, span] = (
             y_ref[:, span]
             + before * carry_ref[:, span]
             + wide8[2:3, span] * conv[:, span].astype(F32)
-        ).astype(BF16)
+        )
+
+    turned = []
+
+    def gate_piece(p):
+        span = span_of(p)
+        part_g[p - 3].wait_recv()
         gate = (own[:, span] + in_g[:, span].astype(F32)).astype(BF16).astype(F32)
-        gated[:, span] = (y.astype(F32) * jax.nn.silu(gate)).astype(BF16)
-
-    my_columns = pl.ds(pl.multiple_of(h * width, 128), width)
-    turned = [
-        rdma(
-            gated.at[pl.ds(pl.multiple_of(heads[d] * rows_h, 64), rows_h)],
-            whole.at[:, my_columns],
-            turn_send.at[d],
-            turn_recv.at[d],
-            s,
-            heads[d],
-        )
-        for d in range(3)
-    ]
-    for c in turned:
-        c.start()
-    keep = pltpu.make_async_copy(gated.at[my_tokens], whole.at[:, my_columns], local_sem.at[number + 2])
-    keep.start()
-    keep.wait()
+        y = y_ref[:, span].astype(BF16).astype(F32)
+        gated[:, span] = (y * jax.nn.silu(gate)).astype(BF16)
+        size = span.stop - span.start
+        to_columns = pl.ds(pl.multiple_of(h * width + span.start, 128), size)
+        for d in range(3):
+            their_rows = pl.ds(pl.multiple_of(heads[d] * rows_h, 64), rows_h)
+            copy = rdma(
+                gated.at[their_rows, span],
+                whole.at[:, to_columns],
+                turn_send.at[p - 3, d],
+                turn_recv.at[p - 3, d],
+                s,
+                heads[d],
+            )
+            copy.start()
+            turned.append(copy)
+        keep = pltpu.make_async_copy(
+            gated.at[my_tokens, span], whole.at[:, to_columns], local_sem.at[number + p - 1]
+        )
+        keep.start()
+        kept.append(keep)
+
+    kept = []
+    forward(4)
+    part_g.append(to_partner(4, out_g, in_g))
+    own[:, span_of(4)] = product(0, windows[4])
+    gate_piece(3)
+    forward(5)
+    part_g.append(to_partner(5, out_g, in_g))
+    own[:, span_of(5)] = product(0, windows[5])
+    gate_piece(4)
+    gate_piece(5)
+    for c in kept:
+        c.wait()
     for c in turned:
         c.wait_recv()
     full = whole[...].astype(F32)
     mean = jnp.sum(full * full, axis=1, keepdims=True) / inner
-    out_ref[...] = (full * lax.rsqrt(mean + epsilon) * channel_ref[5:6, 0:inner]).astype(BF16)
+    scale = lax.rsqrt(mean + epsilon)
+    for j in range(inner // narrow):
+        span = slice(j * narrow, (j + 1) * narrow)
+        out_ref[:, span] = (
+            whole[:, span].astype(F32) * scale * norm_ref[j : j + 1, :]
+        ).astype(BF16)
 
     for c in [*to_far, *to_beside, *passed, *hid_over, *hid_own, *hid_pass, *tiles_out, *turned]:
         c.wait_send()
@@ -591,21 +613,11 @@
     width = w_values.shape[1]
     count = step_bias.shape[0]
     narrow = w_states.shape[1] // 2
-    inner = norm_gain.shape[0]
-    per_channel = jnp.concatenate(
-        [
-            conv_weight,
-            conv_bias[None, :],
-            jnp.pad(norm_gain, (0, conv_bias.shape[0] - inner))[None, :],
-            jnp.zeros((2, conv_bias.shape[0]), F32),
-        ],
-        axis=0,
-    )
     depth = 2 * w_values.shape[0]
     channels = width + 2 * narrow
     vmem = pl.BlockSpec(memory_space=pltpu.VMEM)
     smem = pl.BlockSpec(memory_space=pltpu.SMEM)
-    anywhere = pl.BlockSpec(memory_space=pl.ANY)
+    far_memory = pl.BlockSpec(memory_space=pltpu.HBM)
     dma = pltpu.SemaphoreType.DMA
     gated_out, final = pl.pallas_call(
         layer_kernel,
@@ -613,7 +625,7 @@
             jax.ShapeDtypeStruct(hidden.shape, BF16),
             jax.ShapeDtypeStruct((width, narrow), F32),
         ),
-        in_specs=[anywhere] * 3 + [vmem] * 3 + [smem] * 4,
+        in_specs=[far_memory] * 3 + [vmem] * 5 + [smem] * 4,
         out_specs=[vmem] * 2,
         scratch_shapes=[
             pltpu.VMEM((2, 2, rows, depth), BF16),
@@ -627,7 +639,7 @@
             pltpu.VMEM((rows, width), F32),
             pltpu.VMEM((rows, narrow), BF16),
             pltpu.VMEM((4, rows, narrow), BF16),
-            dma((9,)),
+            dma((11,)),
             dma((7, 2)),
             dma((7, 2)),
             dma((3, 6)),
@@ -657,8 +669,8 @@
             dma((1,)),
             dma((3,)),
             dma((3,)),
-            dma((3,)),
-            dma((3,)),
+            dma((3, 3)),
+            dma((3, 3)),
             pltpu.VMEM((w_values.shape[0], narrow), BF16),
             pltpu.VMEM((narrow, width), F32),
         ],
@@ -671,7 +683,9 @@
         w_gates,
         w_states,
         w_steps.T,
-        per_channel,
+        conv_weight,
+        conv_bias.reshape(-1, narrow),
+        norm_gain.reshape(-1, narrow),
         step_bias,
         decay_rate,
         skip_gain,

time: 79.4 us -> 92.3 us (1.16)
  Pallas kernels: 73.7 us -> 88.2 us
  local copies, waits for them, and re-layouts: 4.01 us -> 2.49 us
    pallas_call x1, Pallas kernels: 73.7 us -> 88.2 us  [layer(): pl.pallas_call(layer_kernel, out_shape=(jax.ShapeDtypeStruct(hidden.shape...]
    unnamed x6 -> x4, local copies, waits for them, and re-layouts: 2.5 us -> 2.49 us
where the time goes in v5:
time: 92.3 us; the launch traced here: 91.4 us
  Pallas kernels  88.2 us (96%)
  local copies, waits for them, and re-layouts  2.49 us (3%)
    pallas_call x1, Pallas kernels, layer(): pl.pallas_call(layer_kernel, out_shape=(jax.ShapeDtypeStruct(hidden.shape...  88.2 us
    unnamed x4, local copies, waits for them, and re-layouts  2.49 us

profile of v5, /device:TPU:1, one launch (start us, length us, event | category | flops | bytes accessed | tf_op | source)
XLA Modules:
  0.0 91.4 jit_solution(17797692980283357377)
XLA Ops:
  0.6 88.2 %shard_map.131 = (bf16[64,2560]{1,0:T(8,128)(2,1)}, f32[640,128]{1,0:T(8,128)}) custom-call(bf16[64,2560]{1,0:T(8,128)(2,1)} %hidden_ref.1, bf16[320,640]{1,0:T(8,128)(2,1)} %values_ref.1, bf16[320,640]{1,0:T(8,128)(2,1)} %gates_ref.1, bf16[320,256]{1,0:T(8,128)(2,1)} %states_ref.1, bf16[10,320]{1,0:T(8,128)(2,1)} %bitcast.5, f32[4,2816]{1,0:T(4,128)} %taps_ref.1, ...), custom_call_target="tpu_custom_call" | custom-call | tf_op jit(solution)/shard_map/pallas_call | solution.py:622
  88.9 0.0 copy-start
  88.9 1.8 %copy.16 = bf16[64,2560]{1,0:T(8,128)(2,1)} copy(bf16[64,2560]{1,0:T(8,128)(2,1)} %get-tuple-element.8) | data formatting | bytes 655360
  90.6 0.0 copy-done
  90.6 0.7 copy.17
Async XLA Ops:
  88.9 1.8 %copy-start = (f32[640,128]{1,0:T(8,128)S(1)}, f32[640,128]{1,0:T(8,128)}, u32[]{:S(2)}) copy-start(f32[640,128]{1,0:T(8,128)} %get-tuple-element.5) | copy-start | bytes 983044

commit v6 on v5

--- a/solution.py
+++ b/solution.py
@@ -296,8 +296,8 @@
         part.start()
         return part
 
-    forward(0)
-    forward(1)
+    for p in range(3):
+        forward(p)
     for c in local:
         c.wait()
     for c in hid_own:
@@ -305,8 +305,10 @@
     for c in hid_pass:
         c.wait_recv()
     part_s = to_partner(0, out_s, in_s)
+    part_v = [to_partner(1, out_v, in_v)]
+    forward(3)
+    part_v.append(to_partner(2, out_v, in_v))
     small = product(0, windows[0])
-    part_v = [to_partner(1, out_v, in_v)]
     part_s.wait_recv()
     small = small + in_s[...].astype(F32)
     tile[...] = small.astype(BF16)
@@ -316,7 +318,8 @@
     for c in tiles_out:
         c.start()
     tiles[h] = tile[...]
-    own[:, span_of(1)] = product(0, windows[1])
+    for p in (1, 2):
+        own[:, span_of(p)] = product(0, windows[p])
 
     rows = own.shape[0]
     start = s * rows
@@ -415,9 +418,6 @@
         low = width + half * narrow
         ext[8:, low : low + narrow] = both
         halo_out[:, low : low + narrow] = both[rows - 16 :, :].astype(BF16)
-    forward(2)
-    part_v.append(to_partner(2, out_v, in_v))
-    own[:, span_of(2)] = product(0, windows[2])
     for c in part_v:
         c.wait_recv()
     pre = (own[...] + in_v[...].astype(F32)).astype(BF16)
@@ -428,6 +428,7 @@
     )
     halo.start()
 
+    forward(4)
     halo.wait_recv()
     ext[0:8, :] = halo_in[8:16, :].astype(F32)
     inner = 4 * width
@@ -475,6 +476,7 @@
         for c in next_one:
             c.start()
 
+    forward(5)
     inc[...] = jnp.zeros(inc.shape, F32)
 
     @pl.when(s > 0)
@@ -488,7 +490,6 @@
         local_out[1] = (local_f32[...] + wide8[0:1, :] * inc[...]).astype(BF16)
         next_two.start()
 
-    forward(3)
     met = jnp.where(
         lower & (segment(start + order) == segment(start + across)),
         jnp.dot(read_state, write_turned, preferred_element_type=F32),
@@ -510,8 +511,10 @@
         preferred_element_type=F32,
     )
 
-    part_g = [to_partner(3, out_g, in_g)]
-    own[:, span_of(3)] = product(0, windows[3])
+    part_g = []
+    for p in (3, 4):
+        part_g.append(to_partner(p, out_g, in_g))
+        own[:, span_of(p)] = product(0, windows[p])
 
     @pl.when(s > 1)
     def _():
@@ -558,11 +561,7 @@
         kept.append(keep)
 
     kept = []
-    forward(4)
-    part_g.append(to_partner(4, out_g, in_g))
-    own[:, span_of(4)] = product(0, windows[4])
     gate_piece(3)
-    forward(5)
     part_g.append(to_partner(5, out_g, in_g))
     own[:, span_of(5)] = product(0, windows[5])
     gate_piece(4)

time: 92.3 us -> 81.3 us (0.88)
  the two profiles are of different devices: /device:TPU:1 before, /device:TPU:3 now
where the time goes in v6:
time: 81.3 us; the launch traced here: 81.1 us
  Pallas kernels  78 us (96%)
  local copies, waits for them, and re-layouts  2.49 us (3%)
    pallas_call x1, Pallas kernels, layer(): pl.pallas_call(layer_kernel, out_shape=(jax.ShapeDtypeStruct(hidden.shape...  78 us
    unnamed x4, local copies, waits for them, and re-layouts  2.49 us

profile of v6, /device:TPU:3, one launch (start us, length us, event | category | flops | bytes accessed | tf_op | source)
XLA Modules:
  0.0 81.1 jit_solution(14988698686873360109)
XLA Ops:
  0.6 78.0 %shard_map.131 = (bf16[64,2560]{1,0:T(8,128)(2,1)}, f32[640,128]{1,0:T(8,128)}) custom-call(bf16[64,2560]{1,0:T(8,128)(2,1)} %hidden_ref.1, bf16[320,640]{1,0:T(8,128)(2,1)} %values_ref.1, bf16[320,640]{1,0:T(8,128)(2,1)} %gates_ref.1, bf16[320,256]{1,0:T(8,128)(2,1)} %states_ref.1, bf16[10,320]{1,0:T(8,128)(2,1)} %bitcast.5, f32[4,2816]{1,0:T(4,128)} %taps_ref.1, ...), custom_call_target="tpu_custom_call" | custom-call | tf_op jit(solution)/shard_map/pallas_call | solution.py:621
  78.6 0.0 copy-start
  78.6 1.8 %copy.16 = bf16[64,2560]{1,0:T(8,128)(2,1)} copy(bf16[64,2560]{1,0:T(8,128)(2,1)} %get-tuple-element.8) | data formatting | bytes 655360
  80.4 0.0 copy-done
  80.4 0.7 copy.17
Async XLA Ops:
  78.6 1.8 %copy-start = (f32[640,128]{1,0:T(8,128)S(1)}, f32[640,128]{1,0:T(8,128)}, u32[]{:S(2)}) copy-start(f32[640,128]{1,0:T(8,128)} %get-tuple-element.5) | copy-start | bytes 983044

commit v7 on v4

--- a/solution.py
+++ b/solution.py
@@ -64,7 +64,9 @@
     gates_ref,
     states_ref,
     steps_ref,
-    channel_ref,
+    taps_ref,
+    offset_ref,
+    norm_ref,
     bias_ref,
     decay_ref,
     skip_ref,
@@ -442,10 +444,12 @@
         low = j * narrow
         if low < width:
             from_lane = pl.ds(pl.multiple_of(h * width + low, 128), narrow)
+            offset = offset_ref[pl.ds(h * (width // narrow) + j, 1), :]
         else:
             from_lane = pl.ds(inner + low - width, narrow)
-        taps = channel_ref[:, from_lane]
-        total = jnp.zeros((rows, narrow), F32) + taps[4:5, :]
+            offset = offset_ref[pl.ds((inner + low - width) // narrow, 1), :]
+        taps = taps_ref[:, from_lane]
+        total = jnp.zeros((rows, narrow), F32) + offset
         for tap in range(4):
             piece = ext[5 + tap : 5 + tap + rows, low : low + narrow] * taps[tap : tap + 1, :]
             total = total + (piece * same[tap] if tap < 3 else piece)
@@ -556,7 +560,12 @@
         c.wait_recv()
     full = whole[...].astype(F32)
     mean = jnp.sum(full * full, axis=1, keepdims=True) / inner
-    out_ref[...] = (full * lax.rsqrt(mean + epsilon) * channel_ref[5:6, 0:inner]).astype(BF16)
+    scale = lax.rsqrt(mean + epsilon)
+    for j in range(inner // narrow):
+        span = slice(j * narrow, (j + 1) * narrow)
+        out_ref[:, span] = (
+            whole[:, span].astype(F32) * scale * norm_ref[j : j + 1, :]
+        ).astype(BF16)
 
     for c in [*to_far, *to_beside, *passed, *hid_over, *hid_own, *hid_pass, *tiles_out, *turned]:
         c.wait_send()
@@ -592,15 +601,6 @@
     count = step_bias.shape[0]
     narrow = w_states.shape[1] // 2
     inner = norm_gain.shape[0]
-    per_channel = jnp.concatenate(
-        [
-            conv_weight,
-            conv_bias[None, :],
-            jnp.pad(norm_gain, (0, conv_bias.shape[0] - inner))[None, :],
-            jnp.zeros((2, conv_bias.shape[0]), F32),
-        ],
-        axis=0,
-    )
     depth = 2 * w_values.shape[0]
     channels = width + 2 * narrow
     vmem = pl.BlockSpec(memory_space=pltpu.VMEM)
@@ -613,7 +613,7 @@
             jax.ShapeDtypeStruct(hidden.shape, BF16),
             jax.ShapeDtypeStruct((width, narrow), F32),
         ),
-        in_specs=[anywhere] * 3 + [vmem] * 3 + [smem] * 4,
+        in_specs=[anywhere] * 3 + [vmem] * 5 + [smem] * 4,
         out_specs=[vmem] * 2,
         scratch_shapes=[
             pltpu.VMEM((2, 2, rows, depth), BF16),
@@ -671,7 +671,9 @@
         w_gates,
         w_states,
         w_steps.T,
-        per_channel,
+        conv_weight,
+        conv_bias.reshape(-1, narrow),
+        norm_gain.reshape(-1, narrow),
         step_bias,
         decay_rate,
         skip_gain,

time: 79.4 us -> 77 us (0.970)
  local copies, waits for them, and re-layouts: 4.01 us -> 2.49 us
    unnamed x6 -> x4, local copies, waits for them, and re-layouts: 2.5 us -> 2.49 us
where the time goes in v7:
time: 77 us; the launch traced here: 76.8 us
  Pallas kernels  73.7 us (96%)
  local copies, waits for them, and re-layouts  2.49 us (3%)
    pallas_call x1, Pallas kernels, layer(): pl.pallas_call(layer_kernel, out_shape=(jax.ShapeDtypeStruct(hidden.shape...  73.7 us
    unnamed x4, local copies, waits for them, and re-layouts  2.49 us

profile of v7, /device:TPU:1, one launch (start us, length us, event | category | flops | bytes accessed | tf_op | source)
XLA Modules:
  0.0 76.8 jit_solution(16004358826638669377)
XLA Ops:
  0.6 73.7 %shard_map.131 = (bf16[64,2560]{1,0:T(8,128)(2,1)}, f32[640,128]{1,0:T(8,128)}) custom-call(bf16[64,2560]{1,0:T(8,128)(2,1)} %hidden_ref.1, bf16[320,640]{1,0:T(8,128)(2,1)} %values_ref.1, bf16[320,640]{1,0:T(8,128)(2,1)} %gates_ref.1, bf16[320,256]{1,0:T(8,128)(2,1)} %states_ref.1, bf16[10,320]{1,0:T(8,128)(2,1)} %bitcast.5, f32[4,2816]{1,0:T(4,128)} %taps_ref.1, ...), custom_call_target="tpu_custom_call" | custom-call | tf_op jit(solution)/shard_map/pallas_call | solution.py:610
  74.3 0.0 copy-start
  74.4 1.8 %copy.16 = bf16[64,2560]{1,0:T(8,128)(2,1)} copy(bf16[64,2560]{1,0:T(8,128)(2,1)} %get-tuple-element.8) | data formatting | bytes 655360
  76.1 0.0 copy-done
  76.1 0.7 copy.17
Async XLA Ops:
  74.3 1.8 %copy-start = (f32[640,128]{1,0:T(8,128)S(1)}, f32[640,128]{1,0:T(8,128)}, u32[]{:S(2)}) copy-start(f32[640,128]{1,0:T(8,128)} %get-tuple-element.5) | copy-start | bytes 983044
